TPU v7x, 128 devices: a whole 4x4x4 slice. The times are simulated.
128 devices in a mesh: lat: 8 (over z_lo, x), lon: 16 (over y, z_hi, core).
Axes of the slice: x: 4, y: 4, z: 4 (z_hi: 2, z_lo: 2; z = z_hi * 2 + z_lo), core: 2. Of those that a mesh axis runs over, the one named last changes fastest.
Arguments:
- queries: bfloat16 [1, 64, 256, 1024], P(None, 'lat', 'lon'), may hold values from -180 to 180
- key_vectors: bfloat16 [1, 64, 256, 1024], P(None, 'lat', 'lon'), may hold values from -4.5 to 4.5
- value_vectors: bfloat16 [1, 64, 256, 1024], P(None, 'lat', 'lon'), may hold values from -6 to 6
- cotangent: bfloat16 [1, 64, 256, 1024], P(None, 'lat', 'lon'), may hold values from -6 to 6
- neighbour_lists: int32 [8, 16], replicated, may hold values from 0 to 15, as said below
- list_counts: int32 [8], replicated, may hold values from 3 to 16, as said below
Outputs:
- attended: bfloat16 [1, 64, 256, 1024], P(None, 'lat', 'lon')
- query_grad: bfloat16 [1, 64, 256, 1024], P(None, 'lat', 'lon')
- key_grad: bfloat16 [1, 64, 256, 1024], P(None, 'lat', 'lon')
- value_grad: bfloat16 [1, 64, 256, 1024], P(None, 'lat', 'lon')
Inputs may be any that keep to these rules, and one draw needn't show every extreme that they name: `neighbour_lists`: the first list_counts[b] entries of row b are distinct cycle offsets and always include 0, 1 and 15; later entries are padding and name nothing. `list_counts`: band 0 and band 8 - 1 list all 16 offsets.
All inputs are finite; a program needn't handle non-finite values.
Results may differ from a plain program's by a relative error of at most 0.03.
Values may be sent and summed in bfloat16 or wider, within the bound.
No kernel may reach another device: no remote copies, remote signals or barrier semaphores. Data moves between devices by JAX's collectives and lax.ppermute only.
A program may use at most 128 MiB of HBM per device.

v0:
```python
import jax
import jax.numpy as jnp
from jax import lax
from jax.experimental import pallas as pl
from jax.experimental.pallas import tpu as pltpu
from jax.sharding import PartitionSpec as P

HEADS = 16
HEAD_DIM = 64
PAIR = 2 * HEAD_DIM
SCALE = HEAD_DIM ** (-0.5)
LOG2E = 1.4426950408889634
MASKED = -1e30
BF16 = jnp.bfloat16
F32 = jnp.float32
NN = (((1,), (0,)), ((), ()))
NT = (((1,), (1,)), ((), ()))
VMEM = pl.BlockSpec(memory_space=pltpu.VMEM)
SMEM = pl.BlockSpec(memory_space=pltpu.SMEM)


def dot(a, b, dims=NN):
    return lax.dot_general(a, b, dims, preferred_element_type=F32)


def pack_pairs(first_ref, second_ref, out_ref):
    for head in range(HEADS):
        lanes = slice(head * HEAD_DIM, (head + 1) * HEAD_DIM)
        out_ref[head] = jnp.concatenate([first_ref[:, lanes], second_ref[:, lanes]], axis=1)


def pack_kv_kernel(key_ref, value_ref, kv_ref):
    pack_pairs(key_ref, value_ref, kv_ref)


def pack_qc_kernel(lists_ref, counts_ref, query_ref, cot_ref, qc_ref, bias_ref):
    pack_pairs(query_ref, cot_ref, qc_ref)
    band = lax.axis_index("lat")
    bands = lists_ref.shape[0]
    slots = lists_ref.shape[1]
    sectors = bias_ref.shape[0] - 2
    shape = (sectors, bias_ref.shape[1])
    cells = shape[1] // sectors
    key_sector = lax.broadcasted_iota(jnp.int32, shape, 0)
    query_sector = lax.broadcasted_iota(jnp.int32, shape, 1) // cells
    offset = key_sector - query_sector
    offset = jnp.where(offset < 0, offset + sectors, offset)
    count = counts_ref[band]
    bias = jnp.full(shape, MASKED, F32)
    for slot in range(slots):
        named = jnp.where(slot < count, lists_ref[band, slot], -1)
        bias = jnp.where(offset == named, 0.0, bias)
    bias_ref[:sectors] = bias
    below = jnp.where(band > 0, 0.0, MASKED).astype(F32)
    above = jnp.where(band < bands - 1, 0.0, MASKED).astype(F32)
    row = lax.broadcasted_iota(jnp.int32, (2, shape[1]), 0)
    bias_ref[sectors:] = jnp.where(row == 0, below, above)


def lane_scale():
    lane = lax.broadcasted_iota(jnp.int32, (1, PAIR), 1)
    return jnp.where(lane < HEAD_DIM, SCALE, 1.0).astype(F32)


def attend_kernel(
    kv_ref, qc_ref, low_ref, high_ref, bias_ref,
    out_ref, grad_ref, low_grad_ref, high_grad_ref,
    kv_t, scores, terms,
):
    sectors, cells, _ = kv_ref.shape
    chunks = sectors // 2
    wide = 2 * cells
    for sector in range(sectors):
        kv_t[:, sector * cells : (sector + 1) * cells] = kv_ref[sector].T
    grad_ref[...] = jnp.zeros_like(grad_ref)
    halves = [slice(a * cells, (a + 1) * cells) for a in range(2)]

    def chunk(t, carry):
        lanes = pl.ds(pl.multiple_of(t * wide, wide), wide)
        qc_t = qc_ref[pl.ds(2 * t, 2)].reshape(wide, PAIR).T
        zeros = jnp.zeros((HEAD_DIM, wide), BF16)
        queries = jnp.concatenate([qc_t[:HEAD_DIM], zeros], axis=0)
        rims = [
            jnp.concatenate([low_ref[2 * t + a], high_ref[2 * t + a]], axis=0) for a in range(2)
        ]
        rims_t = [rim.T for rim in rims]

        def against(block, right):
            if block < chunks:
                return dot(kv_ref[2 * block : 2 * block + 2].reshape(wide, PAIR), right)
            return jnp.concatenate(
                [dot(rims[a], right[:, halves[a]]) for a in range(2)], axis=1
            )

        def gathered(block, part, right):
            rows = slice(block * wide, (block + 1) * wide)
            if block < chunks:
                return dot(kv_t[part, rows], right)
            return jnp.concatenate(
                [dot(rims_t[a][part], right[:, halves[a]]) for a in range(2)], axis=1
            )

        highest = jnp.full((8, wide), -jnp.inf, F32)
        for block in range(chunks + 1):
            rows = slice(block * wide, (block + 1) * wide)
            s = against(block, queries).reshape(2, cells, wide)
            s = s + bias_ref[2 * block : 2 * block + 2, lanes].reshape(2, 1, wide)
            s = s.reshape(wide, wide)
            scores[rows, :] = s
            highest = jnp.maximum(highest, jnp.max(s.reshape(wide // 8, 8, wide), axis=0))
        highest = jnp.max(highest, axis=0, keepdims=True)

        total = jnp.zeros((8, wide), F32)
        out_t = jnp.zeros((HEAD_DIM, wide), F32)
        for block in range(chunks + 1):
            rows = slice(block * wide, (block + 1) * wide)
            p = jnp.exp2((scores[rows, :] - highest) * (SCALE * LOG2E))
            total = total + jnp.sum(p.reshape(wide // 8, 8, wide), axis=0)
            scores[rows, :] = p
            p_low = p.astype(BF16)
            terms[rows, :wide] = p_low
            out_t = out_t + gathered(block, slice(HEAD_DIM, PAIR), p_low)
        inverse = 1.0 / jnp.sum(total, axis=0, keepdims=True)
        out_low = (out_t * inverse).astype(BF16)
        cot_t = (qc_t[HEAD_DIM:].astype(F32) * inverse).astype(BF16)
        spread = jnp.sum(cot_t.astype(F32) * out_low.astype(F32), axis=0, keepdims=True)
        cots = jnp.concatenate([zeros, cot_t], axis=0)
        both = jnp.concatenate([cots, queries], axis=1)

        query_t = jnp.zeros((HEAD_DIM, wide), F32)
        for block in range(chunks + 1):
            rows = slice(block * wide, (block + 1) * wide)
            slopes = (scores[rows, :] * (against(block, cots) - spread)).astype(BF16)
            terms[rows, wide:] = slopes
            query_t = query_t + gathered(block, slice(0, HEAD_DIM), slopes)
            if block < chunks:
                grad = dot(terms[rows, :], both, NT)
                grad_ref[2 * block : 2 * block + 2] += grad.reshape(2, cells, PAIR)
            else:
                for a in range(2):
                    left = jnp.concatenate([terms[rows, halves[a]], slopes[:, halves[a]]], axis=1)
                    right = jnp.concatenate([cots[:, halves[a]], queries[:, halves[a]]], axis=1)
                    grad = dot(left, right, NT) * lane_scale()
                    low_grad_ref[2 * t + a] = grad[:cells].astype(BF16)
                    high_grad_ref[2 * t + a] = grad[cells:].astype(BF16)
        packed = jnp.concatenate([(query_t * SCALE).astype(BF16), out_low], axis=0)
        out_ref[pl.ds(2 * t, 2)] = packed.T.reshape(2, cells, PAIR)
        return carry

    lax.fori_loop(0, chunks, chunk, 0)
    grad_ref[...] = grad_ref[...] * lane_scale().reshape(1, 1, PAIR)


def unpack_kernel(out_ref, grad_ref, attended_ref, query_ref, key_ref, value_ref):
    for head in range(0, HEADS, 2):
        lanes = slice(head * HEAD_DIM, (head + 2) * HEAD_DIM)
        for pair_ref, first_ref, second_ref in (
            (out_ref, query_ref, attended_ref),
            (grad_ref, key_ref, value_ref),
        ):
            one, two = pair_ref[head], pair_ref[head + 1]
            first_ref[:, lanes] = jnp.concatenate([one[:, :HEAD_DIM], two[:, :HEAD_DIM]], axis=1)
            second_ref[:, lanes] = jnp.concatenate([one[:, HEAD_DIM:], two[:, HEAD_DIM:]], axis=1)


def cost(flops, nbytes):
    return pl.CostEstimate(flops=flops, bytes_accessed=nbytes, transcendentals=0)


def per_device(queries, key_vectors, value_vectors, cotangent, neighbour_lists, list_counts):
    _, band_rows, cycle_cols, features = queries.shape
    cells = band_rows * cycle_cols
    sectors = lax.axis_size("lon")
    bands = lax.axis_size("lat")
    flat = (cells, features)
    by_head = jax.ShapeDtypeStruct((HEADS, cells, PAIR), BF16)
    by_sector = jax.ShapeDtypeStruct((sectors, cells, PAIR), BF16)
    key_rows = (sectors + 2) * cells

    kv = pl.pallas_call(
        pack_kv_kernel, out_shape=by_head, in_specs=[VMEM] * 2, out_specs=VMEM,
        cost_estimate=cost(0, 1 << 20), name="pack_kv",
    )(key_vectors.reshape(flat), value_vectors.reshape(flat))
    qc, bias = pl.pallas_call(
        pack_qc_kernel,
        out_shape=(by_head, jax.ShapeDtypeStruct((sectors + 2, sectors * cells), F32)),
        in_specs=[SMEM] * 2 + [VMEM] * 2, out_specs=(VMEM,) * 2,
        cost_estimate=cost(0, 1 << 20), name="pack_qc",
    )(neighbour_lists, list_counts, queries.reshape(flat), cotangent.reshape(flat))

    kv = lax.all_to_all(kv, "lon", 0, 0, tiled=True)
    up = [(band, (band + 1) % bands) for band in range(bands)]
    down = [(target, source) for source, target in up]
    low = lax.ppermute(kv, "lat", up)
    high = lax.ppermute(kv, "lat", down)
    qc = lax.all_to_all(qc, "lon", 0, 0, tiled=True)

    out, grad, low_grad, high_grad = pl.pallas_call(
        attend_kernel,
        out_shape=(by_sector, jax.ShapeDtypeStruct(by_sector.shape, F32), by_sector, by_sector),
        in_specs=[VMEM] * 5, out_specs=(VMEM,) * 4,
        scratch_shapes=[
            pltpu.VMEM((PAIR, sectors * cells), BF16),
            pltpu.VMEM((key_rows, 2 * cells), F32),
            pltpu.VMEM((key_rows, 4 * cells), BF16),
        ],
        compiler_params=pltpu.CompilerParams(vmem_limit_bytes=40 * 1024 * 1024),
        cost_estimate=cost(25 * 10**9, 8 << 20), name="attend",
    )(kv, qc, low, high, bias)

    from_high = lax.ppermute(low_grad, "lat", down)
    from_low = lax.ppermute(high_grad, "lat", up)
    out = lax.all_to_all(out, "lon", 0, 0, tiled=True)
    grad = (grad + from_high.astype(F32) + from_low.astype(F32)).astype(BF16)
    grad = lax.all_to_all(grad, "lon", 0, 0, tiled=True)

    flat_shape = jax.ShapeDtypeStruct(flat, BF16)
    results = pl.pallas_call(
        unpack_kernel, out_shape=(flat_shape,) * 4, in_specs=[VMEM] * 2, out_specs=(VMEM,) * 4,
        cost_estimate=cost(0, 2 << 20), name="unpack",
    )(out, grad)
    return tuple(result.reshape(queries.shape) for result in results)


def solution(mesh):
    blocks = P(None, "lat", "lon", None)
    return jax.shard_map(
        per_device, mesh=mesh, in_specs=(blocks,) * 4 + (P(), P()), out_specs=(blocks,) * 4,
        check_vma=False,
    )
```

profile of v0, /device:TPU:1, one launch (start us, length us, event | category | flops | bytes accessed | tf_op | source)
XLA Modules:
  0.0 116.3 jit_solution(3119272182198170688)
XLA Ops:
  0.6 2.0 %pack_kv.1 = bf16[16,128,128]{2,1,0:T(8,128)(2,1)} custom-call(bf16[128,1024]{1,0:T(8,128)(2,1)} %bitcast.10, bf16[128,1024]{1,0:T(8,128)(2,1)} %bitcast.11), custom_call_target="tpu_custom_call" | custom-call | bytes 1048576 | tf_op jit(solution)/shard_map/pack_kv/pallas_call | solution.py:180
  2.7 20.4 %all_to_all.20.kv_ref = bf16[16,128,128]{2,1,0:T(8,128)(2,1)S(1)} all-to-all(bf16[16,128,128]{2,1,0:T(8,128)(2,1)} %pack_kv.1), channel_id=1, replica_groups=mesh['lat'=8,'lon'=16] {'lon'}, dimensions={0} | all-to-all | bytes 1048576 | tf_op jit(solution)/shard_map/all_to_all | solution.py:191
  23.1 2.9 %collective-permute-start.1 = (bf16[16,128,128]{2,1,0:T(8,128)(2,1)S(1)}, bf16[16,128,128]{2,1,0:T(8,128)(2,1)S(1)}, u32[]{:S(2)}, u32[]{:S(2)}) collective-permute-start(bf16[16,128,128]{2,1,0:T(8,128)(2,1)S(1)} %all_to_all.20.kv_ref), channel_id=1, source_target_pairs={{16,0},{32,16},{48,32},{64,48},{80,64},{96,80},{112,96},{0,112},{1... | collective-permute-start | bytes 1572872 | tf_op jit(solution)/shard_map/ppermute | solution.py:195
  26.0 0.0 collective-permute-start
  26.0 2.2 %pack_qc.1 = (bf16[16,128,128]{2,1,0:T(8,128)(2,1)}, f32[18,2048]{1,0:T(8,128)}) custom-call(s32[8,16]{1,0:T(8,128)} %lists_ref.1, s32[8]{0:T(128)} %counts_ref.1, bf16[128,1024]{1,0:T(8,128)(2,1)} %bitcast.8, bf16[128,1024]{1,0:T(8,128)(2,1)} %bitcast.9), custom_call_target="tpu_custom_call" | custom-call | bytes 1048576 | tf_op jit(solution)/shard_map/pack_qc/pallas_call | solution.py:184
  28.2 0.0 copy-start.2
  28.2 19.9 %all_to_all.21.qc_ref = bf16[16,128,128]{2,1,0:T(8,128)(2,1)S(1)} all-to-all(bf16[16,128,128]{2,1,0:T(8,128)(2,1)} %get-tuple-element.14), channel_id=1, replica_groups=mesh['lat'=8,'lon'=16] {'lon'}, dimensions={0} | all-to-all | bytes 1048576 | tf_op jit(solution)/shard_map/all_to_all | solution.py:196
  48.1 0.0 collective-permute-done.1.high_ref
  48.1 0.0 collective-permute-done.low_ref
  48.1 0.0 copy-start
  48.1 0.8 copy-done
  48.9 0.0 copy-done.2
  48.9 0.0 copy-start.1
  48.9 1.0 copy-done.1
  50.0 25.4 %attend.1 = (bf16[16,128,128]{2,1,0:T(8,128)(2,1)}, f32[16,128,128]{2,1,0:T(8,128)S(1)}, bf16[16,128,128]{2,1,0:T(8,128)(2,1)S(1)}, bf16[16,128,128]{2,1,0:T(8,128)(2,1)S(1)}) custom-call(bf16[16,128,128]{2,1,0:T(8,128)(2,1)S(1)} %all_to_all.20.kv_ref, bf16[16,128,128]{2,1,0:T(8,128)(2,1)S(1)} %all_to_all.21.qc_ref, bf16[16,128,128]{2,1,0:T(8,128)(2,1)S(1)} %copy-done.1, ...), custom_call_target="tpu_custom_call" | custom-call | flops 24999999488 | bytes 8388608 | tf_op jit(solution)/shard_map/attend/pallas_call | solution.py:198
  75.4 0.2 collective-permute-start.2
  75.6 1.3 %collective-permute-start.3 = (bf16[16,128,128]{2,1,0:T(8,128)(2,1)S(1)}, bf16[16,128,128]{2,1,0:T(8,128)(2,1)}, u32[]{:S(2)}, u32[]{:S(2)}) collective-permute-start(bf16[16,128,128]{2,1,0:T(8,128)(2,1)S(1)} %get-tuple-element.19), channel_id=1, source_target_pairs={{0,16},{16,32},{32,48},{48,64},{64,80},{80,96},{96,112},{112,0},{1... | collective-permute-start | bytes 1572872 | tf_op jit(solution)/shard_map/ppermute | solution.py:212
  76.8 5.6 %all-to-all-start.2 = ((bf16[16,128,128]{2,1,0:T(8,128)(2,1)}), bf16[16,128,128]{2,1,0:T(8,128)(2,1)S(1)}, u32[]{:S(2)}, u32[]{:S(2)}) async-start(bf16[16,128,128]{2,1,0:T(8,128)(2,1)} %get-tuple-element.16), calls=%async_computation.2 | async-start | bytes 1048576 | tf_op jit(solution)/shard_map/all_to_all | solution.py:213
  82.5 6.1 %collective-permute-done.2 = bf16[16,128,128]{2,1,0:T(8,128)(2,1)S(1)} collective-permute-done((bf16[16,128,128]{2,1,0:T(8,128)(2,1)S(1)}, bf16[16,128,128]{2,1,0:T(8,128)(2,1)S(1)}, u32[]{:S(2)}, u32[]{:S(2)}) %collective-permute-start.2) | collective-permute-done | bytes 524320 | tf_op jit(solution)/shard_map/ppermute | solution.py:211
  88.6 2.6 %collective-permute-done.3 = bf16[16,128,128]{2,1,0:T(8,128)(2,1)} collective-permute-done((bf16[16,128,128]{2,1,0:T(8,128)(2,1)S(1)}, bf16[16,128,128]{2,1,0:T(8,128)(2,1)}, u32[]{:S(2)}, u32[]{:S(2)}) %collective-permute-start.3) | collective-permute-done | bytes 524320 | tf_op jit(solution)/shard_map/ppermute | solution.py:212
  91.2 1.2 %add_convert_fusion = bf16[16,128,128]{2,1,0:T(8,128)(2,1)S(1)} fusion(bf16[16,128,128]{2,1,0:T(8,128)(2,1)} %collective-permute-done.3, f32[16,128,128]{2,1,0:T(8,128)S(1)} %get-tuple-element.17, bf16[16,128,128]{2,1,0:T(8,128)(2,1)S(1)} %collective-permute-done.2), kind=kLoop, calls=%fused_computation | loop fusion | flops 1310720 | bytes 2621440 | tf_op jit(solution)/shard_map/convert_element_type | solution.py:214
  92.4 6.3 %all-to-all-done.2.out_ref = bf16[16,128,128]{2,1,0:T(8,128)(2,1)S(1)} async-done(((bf16[16,128,128]{2,1,0:T(8,128)(2,1)}), bf16[16,128,128]{2,1,0:T(8,128)(2,1)S(1)}, u32[]{:S(2)}, u32[]{:S(2)}) %all-to-all-start.2) | async-done | bytes 524320 | tf_op jit(solution)/shard_map/all_to_all | solution.py:213
  98.7 0.0 copy-start.3
  98.7 15.1 %all_to_all.22.grad_ref = bf16[16,128,128]{2,1,0:T(8,128)(2,1)} all-to-all(bf16[16,128,128]{2,1,0:T(8,128)(2,1)S(1)} %add_convert_fusion), channel_id=1, replica_groups=mesh['lat'=8,'lon'=16] {'lon'}, dimensions={0} | all-to-all | bytes 1048576 | tf_op jit(solution)/shard_map/all_to_all | solution.py:215
  113.8 0.0 copy-done.3
  113.8 2.5 %unpack.1 = (bf16[128,1024]{1,0:T(8,128)(2,1)}, bf16[128,1024]{1,0:T(8,128)(2,1)}, bf16[128,1024]{1,0:T(8,128)(2,1)}, bf16[128,1024]{1,0:T(8,128)(2,1)}) custom-call(bf16[16,128,128]{2,1,0:T(8,128)(2,1)} %copy-done.3, bf16[16,128,128]{2,1,0:T(8,128)(2,1)} %all_to_all.22.grad_ref), custom_call_target="tpu_custom_call" | custom-call | bytes 2097152 | tf_op jit(solution)/shard_map/unpack/pallas_call | solution.py:218
Async XLA Ops:
  23.1 25.0 %collective-permute-start.1 = (bf16[16,128,128]{2,1,0:T(8,128)(2,1)S(1)}, bf16[16,128,128]{2,1,0:T(8,128)(2,1)S(1)}, u32[]{:S(2)}, u32[]{:S(2)}) collective-permute-start(bf16[16,128,128]{2,1,0:T(8,128)(2,1)S(1)} %all_to_all.20.kv_ref), channel_id=1, source_target_pairs={{16,0},{32,16},{48,32},{64,48},{80,64},{96,80},{112,96},{0,112},{1... | collective-permute-start | bytes 1572872 | tf_op jit(solution)/shard_map/ppermute | solution.py:195
  26.0 22.1 %collective-permute-start = (bf16[16,128,128]{2,1,0:T(8,128)(2,1)S(1)}, bf16[16,128,128]{2,1,0:T(8,128)(2,1)S(1)}, u32[]{:S(2)}, u32[]{:S(2)}) collective-permute-start(bf16[16,128,128]{2,1,0:T(8,128)(2,1)S(1)} %all_to_all.20.kv_ref), channel_id=1, source_target_pairs={{0,16},{16,32},{32,48},{48,64},{64,80},{80,96},{96,112},{112,0},{1... | collective-permute-start | bytes 1572872 | tf_op jit(solution)/shard_map/ppermute | solution.py:194
  28.2 20.7 %copy-start.2 = (f32[18,2048]{1,0:T(8,128)S(1)}, f32[18,2048]{1,0:T(8,128)}, u32[]{:S(2)}) copy-start(f32[18,2048]{1,0:T(8,128)} %get-tuple-element.15.bias_ref) | copy-start | bytes 442372
  48.1 0.8 copy-start
  48.9 1.0 copy-start.1
  75.4 13.2 %collective-permute-start.2 = (bf16[16,128,128]{2,1,0:T(8,128)(2,1)S(1)}, bf16[16,128,128]{2,1,0:T(8,128)(2,1)S(1)}, u32[]{:S(2)}, u32[]{:S(2)}) collective-permute-start(bf16[16,128,128]{2,1,0:T(8,128)(2,1)S(1)} %get-tuple-element.18), channel_id=1, source_target_pairs={{16,0},{32,16},{48,32},{64,48},{80,64},{96,80},{112,96},{0,112},{1... | collective-permute-start | bytes 1572872 | tf_op jit(solution)/shard_map/ppermute | solution.py:211
  75.6 15.6 %collective-permute-start.3 = (bf16[16,128,128]{2,1,0:T(8,128)(2,1)S(1)}, bf16[16,128,128]{2,1,0:T(8,128)(2,1)}, u32[]{:S(2)}, u32[]{:S(2)}) collective-permute-start(bf16[16,128,128]{2,1,0:T(8,128)(2,1)S(1)} %get-tuple-element.19), channel_id=1, source_target_pairs={{0,16},{16,32},{32,48},{48,64},{64,80},{80,96},{96,112},{112,0},{1... | collective-permute-start | bytes 1572872 | tf_op jit(solution)/shard_map/ppermute | solution.py:212
  76.8 21.8 %all-to-all-start.2 = ((bf16[16,128,128]{2,1,0:T(8,128)(2,1)}), bf16[16,128,128]{2,1,0:T(8,128)(2,1)S(1)}, u32[]{:S(2)}, u32[]{:S(2)}) async-start(bf16[16,128,128]{2,1,0:T(8,128)(2,1)} %get-tuple-element.16), calls=%async_computation.2 | async-start | bytes 1048576 | tf_op jit(solution)/shard_map/all_to_all | solution.py:213
  98.7 15.1 %copy-start.3 = (bf16[16,128,128]{2,1,0:T(8,128)(2,1)}, bf16[16,128,128]{2,1,0:T(8,128)(2,1)S(1)}, u32[]{:S(2)}) copy-start(bf16[16,128,128]{2,1,0:T(8,128)(2,1)S(1)} %all-to-all-done.2.out_ref) | copy-start | bytes 1572868
where the time goes:
time: 117 us; the launch traced here: 116 us
  blocking collectives  55.4 us (47%)
  Pallas kernels  32.1 us (27%)
  waiting for transfers between devices  15 us (13%)
  starting transfers between devices  10 us (9%)
  local copies, waits for them, and re-layouts  1.85 us (2%)
  other arithmetic  1.23 us (1%)
    pallas_call x1, Pallas kernels, per_device(): pl.pallas_call(attend_kernel, out_shape=(by_sector, jax.ShapeDtypeStruct(...  25.4 us
    all_to_all x1, blocking collectives, per_device(): kv = lax.all_to_all(kv, 'lon', 0, 0, tiled=True)  20.4 us
    all_to_all x1, blocking collectives, per_device(): qc = lax.all_to_all(qc, 'lon', 0, 0, tiled=True)  19.9 us
    all_to_all x1, blocking collectives, per_device(): grad = lax.all_to_all(grad, 'lon', 0, 0, tiled=True)  15.1 us
    all_to_all x1, waiting for transfers between devices, per_device(): out = lax.all_to_all(out, 'lon', 0, 0, tiled=True)  6.26 us
    ppermute x1, waiting for transfers between devices, per_device(): from_high = lax.ppermute(low_grad, 'lat', down)  6.13 us
    all_to_all x1, starting transfers between devices, per_device(): out = lax.all_to_all(out, 'lon', 0, 0, tiled=True)  5.62 us
    ppermute x1, starting transfers between devices, per_device(): high = lax.ppermute(kv, 'lat', down)  2.93 us
  transfers between devices with their start and end apart: 5, of which 3 were waited for; matrix products, arithmetic and copies ran while one was open for 1% of the time, Pallas kernels for 2%

commit v1 on v0

v1 whole, which is shorter than its diff:
```python
import jax
import jax.numpy as jnp
from jax import lax
from jax.experimental import pallas as pl
from jax.experimental.pallas import tpu as pltpu
from jax.sharding import PartitionSpec as P

HEADS = 16
HEAD_DIM = 64
PAIR = 2 * HEAD_DIM
SCALE = HEAD_DIM ** (-0.5)
LOG2E = 1.4426950408889634
MASKED = -1e30
BF16 = jnp.bfloat16
F32 = jnp.float32
NN = (((1,), (0,)), ((), ()))
NT = (((1,), (1,)), ((), ()))
VMEM = pl.BlockSpec(memory_space=pltpu.VMEM)
SMEM = pl.BlockSpec(memory_space=pltpu.SMEM)


def dot(a, b, dims=NN):
    return lax.dot_general(a, b, dims, preferred_element_type=F32)


def pack_pairs(first_ref, second_ref, out_ref, rows):
    for head in range(HEADS):
        lanes = slice(head * HEAD_DIM, (head + 1) * HEAD_DIM)
        out_ref[head, rows] = jnp.concatenate([first_ref[:, lanes], second_ref[:, lanes]], axis=1)


def pack_kernel(
    lists_ref, counts_ref, key_ref, value_ref, query_ref, cot_ref, packed_ref, bias_ref
):
    cells = key_ref.shape[0]
    pack_pairs(key_ref, value_ref, packed_ref, slice(0, cells))
    pack_pairs(query_ref, cot_ref, packed_ref, slice(cells, 2 * cells))
    band = lax.axis_index("lat")
    bands, slots = lists_ref.shape
    sectors = bias_ref.shape[0] - 2
    shape = (sectors, bias_ref.shape[1])
    key_sector = lax.broadcasted_iota(jnp.int32, shape, 0)
    query_sector = lax.broadcasted_iota(jnp.int32, shape, 1) // cells
    offset = key_sector - query_sector
    offset = jnp.where(offset < 0, offset + sectors, offset)
    count = counts_ref[band]
    bias = jnp.full(shape, MASKED, F32)
    for slot in range(slots):
        named = jnp.where(slot < count, lists_ref[band, slot], -1)
        bias = jnp.where(offset == named, 0.0, bias)
    bias_ref[:sectors] = bias
    below = jnp.where(band > 0, 0.0, MASKED).astype(F32)
    above = jnp.where(band < bands - 1, 0.0, MASKED).astype(F32)
    row = lax.broadcasted_iota(jnp.int32, (2, shape[1]), 0)
    bias_ref[sectors:] = jnp.where(row == 0, below, above)


def lane_scale():
    lane = lax.broadcasted_iota(jnp.int32, (1, PAIR), 1)
    return jnp.where(lane < HEAD_DIM, SCALE, 1.0).astype(F32)


def fold_rows(values, combine):
    return combine(values.reshape(values.shape[0] // 8, 8, values.shape[1]), axis=0)


def forward_kernel(x_ref, bias_ref, weights_ref, highest_ref, total_ref, out_ref, kv_t_ref, scores):
    sectors, both, _ = x_ref.shape
    cells = both // 2
    chunks = sectors // 2
    wide = 2 * cells
    t = pl.program_id(0)

    @pl.when(t == 0)
    def _():
        for sector in range(sectors):
            kv_t_ref[:, sector * cells : (sector + 1) * cells] = x_ref[sector, :cells].T

    lanes = pl.ds(pl.multiple_of(t * wide, wide), wide)
    qc_t = x_ref[pl.ds(2 * t, 2), cells:].reshape(wide, PAIR).T
    queries = jnp.concatenate([qc_t[:HEAD_DIM], jnp.zeros((HEAD_DIM, wide), BF16)], axis=0)
    highest = jnp.full((8, wide), -jnp.inf, F32)
    for block in range(chunks):
        rows = slice(block * wide, (block + 1) * wide)
        s = dot(x_ref[2 * block : 2 * block + 2, :cells].reshape(wide, PAIR), queries)
        s = s.reshape(2, cells, wide)
        s = s + bias_ref[2 * block : 2 * block + 2, lanes].reshape(2, 1, wide)
        s = s.reshape(wide, wide)
        scores[rows, :] = s
        highest = jnp.maximum(highest, fold_rows(s, jnp.max))
    highest = jnp.max(highest, axis=0, keepdims=True)
    total = jnp.zeros((8, wide), F32)
    out_t = jnp.zeros((HEAD_DIM, wide), F32)
    for block in range(chunks):
        rows = slice(block * wide, (block + 1) * wide)
        p = jnp.exp2((scores[rows, :] - highest) * (SCALE * LOG2E))
        total = total + fold_rows(p, jnp.sum)
        p_low = p.astype(BF16)
        weights_ref[0, rows, :] = p_low
        out_t = out_t + dot(kv_t_ref[HEAD_DIM:, rows], p_low)
    highest_ref[0] = highest
    total_ref[0] = jnp.sum(total, axis=0, keepdims=True)
    out_ref[0] = out_t


def rims_kernel(
    x_ref, bias_ref, low_ref, high_ref, highest_ref, total_ref, out_ref,
    attended_ref, cot_ref, spread_ref, query_ref, low_grad_ref, high_grad_ref,
):
    sectors, both, _ = x_ref.shape
    cells = both // 2
    wide = 2 * cells
    t = pl.program_id(0)
    lanes = pl.ds(pl.multiple_of(t * wide, wide), wide)
    qc_t = x_ref[pl.ds(2 * t, 2), cells:].reshape(wide, PAIR).T
    zeros = jnp.zeros((HEAD_DIM, wide), BF16)
    queries = jnp.concatenate([qc_t[:HEAD_DIM], zeros], axis=0)
    halves = [slice(a * cells, (a + 1) * cells) for a in range(2)]
    rims = [jnp.concatenate([low_ref[a], high_ref[a]], axis=0) for a in range(2)]
    rims_t = [rim.T for rim in rims]

    def paired(parts):
        return jnp.concatenate(parts, axis=1)

    s = paired([dot(rims[a], queries[:, halves[a]]) for a in range(2)]).reshape(2, cells, wide)
    s = (s + bias_ref[sectors : sectors + 2, lanes].reshape(2, 1, wide)).reshape(wide, wide)
    own = highest_ref[0]
    highest = jnp.maximum(own, jnp.max(fold_rows(s, jnp.max), axis=0, keepdims=True))
    p = jnp.exp2((s - highest) * (SCALE * LOG2E))
    p_low = p.astype(BF16)
    ratio = jnp.exp2((own - highest) * (SCALE * LOG2E))
    total = ratio * total_ref[0] + jnp.sum(fold_rows(p, jnp.sum), axis=0, keepdims=True)
    inverse = 1.0 / total
    out_t = out_ref[0] * ratio
    out_t = out_t + paired([dot(rims_t[a][HEAD_DIM:], p_low[:, halves[a]]) for a in range(2)])
    attended = (out_t * inverse).astype(BF16)
    attended_ref[0] = attended
    cot_t = qc_t[HEAD_DIM:].astype(F32) * inverse
    own_cot = (cot_t * ratio).astype(BF16)
    cot_ref[0] = own_cot
    spread_ref[0] = jnp.sum(own_cot.astype(F32) * attended.astype(F32), axis=0, keepdims=True)
    cot_t = cot_t.astype(BF16)
    spread = jnp.sum(cot_t.astype(F32) * attended.astype(F32), axis=0, keepdims=True)
    cots = jnp.concatenate([zeros, cot_t], axis=0)
    product = paired([dot(rims[a], cots[:, halves[a]]) for a in range(2)])
    slopes = (p * (product - spread)).astype(BF16)
    query_ref[0] = paired([dot(rims_t[a][:HEAD_DIM], slopes[:, halves[a]]) for a in range(2)])
    for a in range(2):
        left = paired([p_low[:, halves[a]], slopes[:, halves[a]]])
        right = paired([cots[:, halves[a]], queries[:, halves[a]]])
        grad = dot(left, right, NT) * lane_scale()
        low_grad_ref[a] = grad[:cells].astype(BF16)
        high_grad_ref[a] = grad[cells:].astype(BF16)


def backward_kernel(
    x_ref, kv_t_ref, weights_ref, attended_ref, cot_ref, spread_ref, query_ref, out_ref, grad_ref
):
    sectors, both, _ = x_ref.shape
    cells = both // 2
    chunks = sectors // 2
    wide = 2 * cells
    t = pl.program_id(0)

    @pl.when(t == 0)
    def _():
        grad_ref[...] = jnp.zeros_like(grad_ref)

    queries = x_ref[pl.ds(2 * t, 2), cells:].reshape(wide, PAIR).T[:HEAD_DIM]
    zeros = jnp.zeros((HEAD_DIM, wide), BF16)
    queries = jnp.concatenate([queries, zeros], axis=0)
    cots = jnp.concatenate([zeros, cot_ref[0]], axis=0)
    right = jnp.concatenate([cots, queries], axis=1)
    spread = spread_ref[0]
    query_t = query_ref[0]
    for block in range(chunks):
        rows = slice(block * wide, (block + 1) * wide)
        product = dot(x_ref[2 * block : 2 * block + 2, :cells].reshape(wide, PAIR), cots)
        weights = weights_ref[0, rows, :]
        slopes = (weights.astype(F32) * (product - spread)).astype(BF16)
        query_t = query_t + dot(kv_t_ref[:HEAD_DIM, rows], slopes)
        grad = dot(jnp.concatenate([weights, slopes], axis=1), right, NT)
        grad_ref[2 * block : 2 * block + 2] += grad.reshape(2, cells, PAIR)
    packed = jnp.concatenate([(query_t * SCALE).astype(BF16), attended_ref[0]], axis=0)
    out_ref[...] = packed.T.reshape(2, cells, PAIR)

    @pl.when(t == chunks - 1)
    def _():
        grad_ref[...] = grad_ref[...] * lane_scale().reshape(1, 1, PAIR)


def merge_kernel(out_ref, grad_ref, from_low_ref, from_high_ref, merged_ref):
    cells = out_ref.shape[1]
    merged_ref[:, :cells] = out_ref[...]
    grad = grad_ref[...] + from_low_ref[...].astype(F32) + from_high_ref[...].astype(F32)
    merged_ref[:, cells:] = grad.astype(BF16)


def unpack_kernel(merged_ref, attended_ref, query_ref, key_ref, value_ref):
    cells = attended_ref.shape[0]
    for head in range(0, HEADS, 2):
        lanes = slice(head * HEAD_DIM, (head + 2) * HEAD_DIM)
        for rows, first_ref, second_ref in (
            (slice(0, cells), query_ref, attended_ref),
            (slice(cells, 2 * cells), key_ref, value_ref),
        ):
            one, two = merged_ref[head, rows], merged_ref[head + 1, rows]
            first_ref[:, lanes] = jnp.concatenate([one[:, :HEAD_DIM], two[:, :HEAD_DIM]], axis=1)
            second_ref[:, lanes] = jnp.concatenate([one[:, HEAD_DIM:], two[:, HEAD_DIM:]], axis=1)


def cost(flops, nbytes):
    return pl.CostEstimate(flops=flops, bytes_accessed=nbytes, transcendentals=0)


def whole(*shape):
    return pl.BlockSpec(shape, lambda t: (0,) * len(shape))


def step(*shape):
    return pl.BlockSpec(shape, lambda t: (t,) + (0,) * (len(shape) - 1))


def per_device(queries, key_vectors, value_vectors, cotangent, neighbour_lists, list_counts):
    _, band_rows, cycle_cols, features = queries.shape
    cells = band_rows * cycle_cols
    sectors = lax.axis_size("lon")
    bands = lax.axis_size("lat")
    chunks = sectors // 2
    wide = 2 * cells
    keys = sectors * cells
    flat = (cells, features)
    params = pltpu.CompilerParams(vmem_limit_bytes=32 * 1024 * 1024)
    small = pltpu.CompilerParams(vmem_limit_bytes=16 * 1024 * 1024)
    struct = jax.ShapeDtypeStruct
    paired = struct((sectors, cells, PAIR), BF16)

    packed, bias = pl.pallas_call(
        pack_kernel,
        out_shape=(struct((HEADS, wide, PAIR), BF16), struct((sectors + 2, keys), F32)),
        in_specs=[SMEM] * 2 + [VMEM] * 4, out_specs=(VMEM,) * 2,
        cost_estimate=cost(0, 2 << 20), name="pack",
    )(
        neighbour_lists, list_counts, key_vectors.reshape(flat), value_vectors.reshape(flat),
        queries.reshape(flat), cotangent.reshape(flat),
    )
    x = lax.all_to_all(packed, "lon", 0, 0, tiled=True)
    kv = x[:, :cells]
    up = [(band, (band + 1) % bands) for band in range(bands)]
    down = [(target, source) for source, target in up]
    low = lax.ppermute(kv, "lat", up)
    high = lax.ppermute(kv, "lat", down)

    x_spec = whole(sectors, wide, PAIR)
    bias_spec = whole(sectors + 2, keys)
    row = step(1, 1, wide)
    tall = step(1, HEAD_DIM, wide)
    two = step(2, cells, PAIR)
    weights_spec = step(1, keys, wide)
    kv_t_spec = whole(PAIR, keys)
    row_shape = struct((chunks, 1, wide), F32)
    tall_shape = struct((chunks, HEAD_DIM, wide), F32)
    tall_low = struct((chunks, HEAD_DIM, wide), BF16)

    weights, highest, total, out_t, kv_t = pl.pallas_call(
        forward_kernel, grid=(chunks,),
        out_shape=(
            struct((chunks, keys, wide), BF16), row_shape, row_shape, tall_shape,
            struct((PAIR, keys), BF16),
        ),
        in_specs=[x_spec, bias_spec], out_specs=(weights_spec, row, row, tall, kv_t_spec),
        scratch_shapes=[pltpu.VMEM((keys, wide), F32)],
        compiler_params=params, cost_estimate=cost(10**10, 10 << 20), name="forward",
    )(x, bias)
    attended, cot, spread, query_t, low_grad, high_grad = pl.pallas_call(
        rims_kernel, grid=(chunks,),
        out_shape=(tall_low, tall_low, row_shape, tall_shape, paired, paired),
        in_specs=[x_spec, bias_spec, two, two, row, row, tall],
        out_specs=(tall, tall, row, tall, two, two),
        compiler_params=params, cost_estimate=cost(4 * 10**9, 4 << 20), name="rims",
    )(x, bias, low, high, highest, total, out_t)
    from_high = lax.ppermute(low_grad, "lat", down)
    from_low = lax.ppermute(high_grad, "lat", up)
    out, grad = pl.pallas_call(
        backward_kernel, grid=(chunks,),
        out_shape=(paired, struct(paired.shape, F32)),
        in_specs=[x_spec, kv_t_spec, weights_spec, tall, tall, row, tall],
        out_specs=(two, whole(sectors, cells, PAIR)),
        compiler_params=params, cost_estimate=cost(15 * 10**9, 12 << 20), name="backward",
    )(x, kv_t, weights, attended, cot, spread, query_t)
    merged = pl.pallas_call(
        merge_kernel, out_shape=struct((sectors, wide, PAIR), BF16),
        in_specs=[VMEM] * 4, out_specs=VMEM, compiler_params=small, cost_estimate=cost(0, 4 << 20), name="merge",
    )(out, grad, from_low, from_high)
    merged = lax.all_to_all(merged, "lon", 0, 0, tiled=True)
    results = pl.pallas_call(
        unpack_kernel, out_shape=(struct(flat, BF16),) * 4, in_specs=[VMEM], out_specs=(VMEM,) * 4,
        compiler_params=small, cost_estimate=cost(0, 2 << 20), name="unpack",
    )(merged)
    return tuple(result.reshape(queries.shape) for result in results)


def solution(mesh):
    blocks = P(None, "lat", "lon", None)
    return jax.shard_map(
        per_device, mesh=mesh, in_specs=(blocks,) * 4 + (P(), P()), out_specs=(blocks,) * 4,
        check_vma=False,
    )
```

time: 117 us -> 96.5 us (0.82)
  waiting for transfers between devices: 15 us -> 1.21 us
  blocking collectives: 55.4 us -> 49.7 us
  Pallas kernels: 32.1 us -> 37 us
  starting transfers between devices: 10 us -> 6.64 us
  other arithmetic: 1.23 us -> 0 us
    all_to_all x1 -> x0, waiting for transfers between devices: 6.26 us -> none  [per_device(): out = lax.all_to_all(out, 'lon', 0, 0, tiled=True)]
    ppermute x1, waiting for transfers between devices: 6.13 us -> 0.01 us  [per_device(): from_high = lax.ppermute(low_grad, 'lat', down)]
    all_to_all x3 -> x2, blocking collectives: 55.4 us -> 49.7 us  [the longest x1 26 us: per_device(): x = lax.all_to_all(packed, 'lon', 0, 0, tiled=True)]
    all_to_all x1 -> x0, starting transfers between devices: 5.62 us -> none  [per_device(): out = lax.all_to_all(out, 'lon', 0, 0, tiled=True)]
    pallas_call x4 -> x6, Pallas kernels: 32.1 us -> 37 us  [the longest x1 15.3 us: per_device(): pl.pallas_call(backward_kernel, grid=(chunks,), out_shape=(paired, struct...]
    ppermute x1, starting transfers between devices: 0.21 us -> 3.56 us  [per_device(): from_high = lax.ppermute(low_grad, 'lat', down)]
    ppermute x1, waiting for transfers between devices: 2.57 us -> 0.01 us  [per_device(): from_low = lax.ppermute(high_grad, 'lat', up)]
    convert_element_type x1 -> x0, other arithmetic: 1.23 us -> none  [per_device(): grad = (grad + from_high.astype(F32) + from_low.astype(F32)).astype(BF16)]
  transfers between devices with their start and end apart: 5 -> 4, of which waited for: 3 -> 1; matrix products, arithmetic and copies ran while one was open for 1% -> 0% of each run, Pallas kernels for 2% -> 28%
where the time goes in v1:
time: 96.5 us; the launch traced here: 96.2 us
  blocking collectives  49.7 us (52%)
  Pallas kernels  37 us (38%)
  starting transfers between devices  6.64 us (7%)
  waiting for transfers between devices  1.21 us (1%)
  local copies, waits for them, and re-layouts  0.97 us (1%)
    all_to_all x1, blocking collectives, per_device(): x = lax.all_to_all(packed, 'lon', 0, 0, tiled=True)  26 us
    all_to_all x1, blocking collectives, per_device(): merged = lax.all_to_all(merged, 'lon', 0, 0, tiled=True)  23.7 us
    pallas_call x1, Pallas kernels, per_device(): pl.pallas_call(backward_kernel, grid=(chunks,), out_shape=(paired, struct...  15.3 us
    pallas_call x1, Pallas kernels, per_device(): pl.pallas_call(forward_kernel, grid=(chunks,), out_shape=(struct((chunks,...  11.8 us
    pallas_call x1, Pallas kernels, per_device(): pl.pallas_call(rims_kernel, grid=(chunks,), out_shape=(tall_low, tall_low...  5.73 us
    ppermute x1, starting transfers between devices, per_device(): from_high = lax.ppermute(low_grad, 'lat', down)  3.56 us
    ppermute x1, starting transfers between devices, per_device(): high = lax.ppermute(kv, 'lat', down)  3 us
    pallas_call x1, Pallas kernels, per_device(): pl.pallas_call(pack_kernel, out_shape=(struct((HEADS, wide, PAIR), BF16),...  2.63 us
  transfers between devices with their start and end apart: 4, of which 1 were waited for; matrix products, arithmetic and copies ran while one was open for 0% of the time, Pallas kernels for 28%

profile of v1, /device:TPU:1, one launch (start us, length us, event | category | flops | bytes accessed | tf_op | source)
XLA Modules:
  0.0 96.2 jit_solution(16636276305826030877)
XLA Ops:
  0.6 2.6 %pack.1 = (bf16[16,256,128]{2,1,0:T(8,128)(2,1)}, f32[18,2048]{1,0:T(8,128)}) custom-call(s32[8,16]{1,0:T(8,128)} %lists_ref.1, s32[8]{0:T(128)} %counts_ref.1, bf16[128,1024]{1,0:T(8,128)(2,1)} %bitcast.8, bf16[128,1024]{1,0:T(8,128)(2,1)} %bitcast.9, bf16[128,1024]{1,0:T(8,128)(2,1)} %bitcast.10, bf16[128,1024]{1,0:T(8,128)(2,1)} %bitcast.11), custom_call_target="tpu_custom_call" | custom-call | bytes 2097152 | tf_op jit(solution)/shard_map/pack/pallas_call | solution.py:238
  3.3 26.0 %all_to_all.10.x_ref = bf16[16,256,128]{2,1,0:T(8,128)(2,1)S(1)} all-to-all(bf16[16,256,128]{2,1,0:T(8,128)(2,1)} %get-tuple-element.23), channel_id=1, replica_groups=mesh['lat'=8,'lon'=16] {'lon'}, dimensions={0} | all-to-all | bytes 2097152 | tf_op jit(solution)/shard_map/all_to_all | solution.py:247
  29.4 3.0 %collective-permute-start.1 = (bf16[16,128,128]{2,1,0:T(8,128)(2,1)S(1)}, bf16[16,128,128]{2,1,0:T(8,128)(2,1)S(1)}, u32[]{:S(2)}, u32[]{:S(2)}) collective-permute-start(bf16[16,128,128]{2,1,0:T(8,128)(2,1)S(1)} %slice.4), channel_id=1, source_target_pairs={{16,0},{32,16},{48,32},{64,48},{80,64},{96,80},{112,96},{0,112},{1... | collective-permute-start | bytes 1572872 | tf_op jit(solution)/shard_map/ppermute | solution.py:252
  32.4 0.0 collective-permute-start
  32.4 0.0 copy-start
  32.4 0.9 copy-done
  33.3 11.8 %forward.1 = (bf16[8,2048,256]{2,1,0:T(8,128)(2,1)S(1)}, f32[8,1,256]{2,1,0:T(1,128)S(1)}, f32[8,1,256]{2,1,0:T(1,128)S(1)}, f32[8,64,256]{2,1,0:T(8,128)S(1)}, bf16[128,2048]{1,0:T(8,128)(2,1)S(1)}) custom-call(bf16[16,256,128]{2,1,0:T(8,128)(2,1)S(1)} %all_to_all.10.x_ref, f32[18,2048]{1,0:T(8,128)S(1)} %copy-done), custom_call_target="tpu_custom_call" | custom-call | flops 10000000000 | bytes 10485760 | tf_op jit(solution)/shard_map/forward/pallas_call | solution.py:265
  45.1 0.0 collective-permute-done.1.high_ref
  45.1 1.2 %collective-permute-done.low_ref = bf16[16,128,128]{2,1,0:T(8,128)(2,1)S(1)} collective-permute-done((bf16[16,128,128]{2,1,0:T(8,128)(2,1)S(1)}, bf16[16,128,128]{2,1,0:T(8,128)(2,1)S(1)}, u32[]{:S(2)}, u32[]{:S(2)}) %collective-permute-start) | collective-permute-done | bytes 524320 | tf_op jit(solution)/shard_map/ppermute | solution.py:251
  46.3 5.7 %rims.1 = (bf16[8,64,256]{2,1,0:T(8,128)(2,1)S(1)}, bf16[8,64,256]{2,1,0:T(8,128)(2,1)S(1)}, f32[8,1,256]{2,1,0:T(1,128)S(1)}, f32[8,64,256]{2,1,0:T(8,128)S(1)}...) custom-call(bf16[16,256,128]{2,1,0:T(8,128)(2,1)S(1)} %all_to_all.10.x_ref, ...), custom_call_target="tpu_custom_call" | custom-call | flops 4000000000 | bytes 4194304 | tf_op jit(solution)/shard_map/rims/pallas_call | solution.py:275
  52.0 0.1 collective-permute-start.2
  52.1 3.6 %collective-permute-start.3 = (bf16[16,128,128]{2,1,0:T(8,128)(2,1)S(1)}, bf16[16,128,128]{2,1,0:T(8,128)(2,1)S(1)}, u32[]{:S(2)}, u32[]{:S(2)}) collective-permute-start(bf16[16,128,128]{2,1,0:T(8,128)(2,1)S(1)} %get-tuple-element.37), channel_id=1, source_target_pairs={{16,0},{32,16},{48,32},{64,48},{80,64},{96,80},{112,96},{0,112},{1... | collective-permute-start | bytes 1572872 | tf_op jit(solution)/shard_map/ppermute | solution.py:282
  55.7 15.3 %backward.1 = (bf16[16,128,128]{2,1,0:T(8,128)(2,1)S(1)}, f32[16,128,128]{2,1,0:T(8,128)S(1)}) custom-call(bf16[16,256,128]{2,1,0:T(8,128)(2,1)S(1)} %all_to_all.10.x_ref, bf16[128,2048]{1,0:T(8,128)(2,1)S(1)} %get-tuple-element.25.kv_t_ref, bf16[8,2048,256]{2,1,0:T(8,128)(2,1)S(1)} %get-tuple-element.26.weights_ref, ...), custom_call_target="tpu_custom_call" | custom-call | flops 15000000512 | bytes 12582912 | tf_op jit(solution)/shard_map/backward/pallas_call | solution.py:284
  71.0 0.0 collective-permute-done.2.from_low_ref
  71.0 0.0 collective-permute-done.3.from_high_ref
  71.0 0.2 merge.1
  71.2 23.7 %all_to_all.11.merged_ref = bf16[16,256,128]{2,1,0:T(8,128)(2,1)S(1)} all-to-all(bf16[16,256,128]{2,1,0:T(8,128)(2,1)S(1)} %merge.1), channel_id=1, replica_groups=mesh['lat'=8,'lon'=16] {'lon'}, dimensions={0} | all-to-all | bytes 2097152 | tf_op jit(solution)/shard_map/all_to_all | solution.py:295
  94.9 1.3 %unpack.1 = (bf16[128,1024]{1,0:T(8,128)(2,1)}, bf16[128,1024]{1,0:T(8,128)(2,1)}, bf16[128,1024]{1,0:T(8,128)(2,1)}, bf16[128,1024]{1,0:T(8,128)(2,1)}) custom-call(bf16[16,256,128]{2,1,0:T(8,128)(2,1)S(1)} %all_to_all.11.merged_ref), custom_call_target="tpu_custom_call" | custom-call | bytes 2097152 | tf_op jit(solution)/shard_map/unpack/pallas_call | solution.py:296
  (1 shorter events, 0.0 us)
Async XLA Ops:
  29.4 15.7 %collective-permute-start.1 = (bf16[16,128,128]{2,1,0:T(8,128)(2,1)S(1)}, bf16[16,128,128]{2,1,0:T(8,128)(2,1)S(1)}, u32[]{:S(2)}, u32[]{:S(2)}) collective-permute-start(bf16[16,128,128]{2,1,0:T(8,128)(2,1)S(1)} %slice.4), channel_id=1, source_target_pairs={{16,0},{32,16},{48,32},{64,48},{80,64},{96,80},{112,96},{0,112},{1... | collective-permute-start | bytes 1572872 | tf_op jit(solution)/shard_map/ppermute | solution.py:252
  32.4 13.9 %collective-permute-start = (bf16[16,128,128]{2,1,0:T(8,128)(2,1)S(1)}, bf16[16,128,128]{2,1,0:T(8,128)(2,1)S(1)}, u32[]{:S(2)}, u32[]{:S(2)}) collective-permute-start(bf16[16,128,128]{2,1,0:T(8,128)(2,1)S(1)} %slice.4), channel_id=1, source_target_pairs={{0,16},{16,32},{32,48},{48,64},{64,80},{80,96},{96,112},{112,0},{1... | collective-permute-start | bytes 1572872 | tf_op jit(solution)/shard_map/ppermute | solution.py:251
  32.4 0.9 copy-start
  52.0 18.9 %collective-permute-start.2 = (bf16[16,128,128]{2,1,0:T(8,128)(2,1)S(1)}, bf16[16,128,128]{2,1,0:T(8,128)(2,1)S(1)}, u32[]{:S(2)}, u32[]{:S(2)}) collective-permute-start(bf16[16,128,128]{2,1,0:T(8,128)(2,1)S(1)} %get-tuple-element.36), channel_id=1, source_target_pairs={{0,16},{16,32},{32,48},{48,64},{64,80},{80,96},{96,112},{112,0},{1... | collective-permute-start | bytes 1572872 | tf_op jit(solution)/shard_map/ppermute | solution.py:283
  52.1 18.9 %collective-permute-start.3 = (bf16[16,128,128]{2,1,0:T(8,128)(2,1)S(1)}, bf16[16,128,128]{2,1,0:T(8,128)(2,1)S(1)}, u32[]{:S(2)}, u32[]{:S(2)}) collective-permute-start(bf16[16,128,128]{2,1,0:T(8,128)(2,1)S(1)} %get-tuple-element.37), channel_id=1, source_target_pairs={{16,0},{32,16},{48,32},{64,48},{80,64},{96,80},{112,96},{0,112},{1... | collective-permute-start | bytes 1572872 | tf_op jit(solution)/shard_map/ppermute | solution.py:282

commit v2 on v1

v2 whole, which is shorter than its diff:
```python
import jax
import jax.numpy as jnp
from jax import lax
from jax.experimental import pallas as pl
from jax.experimental.pallas import tpu as pltpu
from jax.sharding import PartitionSpec as P

HEADS = 16
HEAD_DIM = 64
PAIR = 2 * HEAD_DIM
SCALE = HEAD_DIM ** (-0.5)
LOG2E = 1.4426950408889634
MASKED = -1e30
CHUNK = 4
BF16 = jnp.bfloat16
F32 = jnp.float32
NN = (((1,), (0,)), ((), ()))
NT = (((1,), (1,)), ((), ()))
VMEM = pl.BlockSpec(memory_space=pltpu.VMEM)
SMEM = pl.BlockSpec(memory_space=pltpu.SMEM)


def dot(a, b, dims=NN):
    return lax.dot_general(a, b, dims, preferred_element_type=F32)


def pack_pairs(first_ref, second_ref, out_ref, rows):
    for head in range(HEADS):
        lanes = slice(head * HEAD_DIM, (head + 1) * HEAD_DIM)
        out_ref[head, rows] = jnp.concatenate([first_ref[:, lanes], second_ref[:, lanes]], axis=1)


def pack_kernel(
    lists_ref, counts_ref, key_ref, value_ref, query_ref, cot_ref, packed_ref, bias_ref
):
    cells = key_ref.shape[0]
    pack_pairs(key_ref, value_ref, packed_ref, slice(0, cells))
    pack_pairs(query_ref, cot_ref, packed_ref, slice(cells, 2 * cells))
    band = lax.axis_index("lat")
    bands, slots = lists_ref.shape
    sectors = bias_ref.shape[0] - 2
    shape = (sectors, bias_ref.shape[1])
    key_sector = lax.broadcasted_iota(jnp.int32, shape, 0)
    query_sector = lax.broadcasted_iota(jnp.int32, shape, 1) // cells
    offset = key_sector - query_sector
    offset = jnp.where(offset < 0, offset + sectors, offset)
    count = counts_ref[band]
    bias = jnp.full(shape, MASKED, F32)
    for slot in range(slots):
        named = jnp.where(slot < count, lists_ref[band, slot], -1)
        bias = jnp.where(offset == named, 0.0, bias)
    bias_ref[:sectors] = bias
    below = jnp.where(band > 0, 0.0, MASKED).astype(F32)
    above = jnp.where(band < bands - 1, 0.0, MASKED).astype(F32)
    row = lax.broadcasted_iota(jnp.int32, (2, shape[1]), 0)
    bias_ref[sectors:] = jnp.where(row == 0, below, above)


def lane_scale():
    lane = lax.broadcasted_iota(jnp.int32, (1, PAIR), 1)
    return jnp.where(lane < HEAD_DIM, SCALE, 1.0).astype(F32)


def fold_rows(values, combine):
    return combine(values.reshape(values.shape[0] // 8, 8, values.shape[1]), axis=0)


def forward_kernel(x_ref, bias_ref, weights_ref, highest_ref, total_ref, out_ref, kv_t_ref, scores):
    sectors, both, _ = x_ref.shape
    cells = both // 2
    chunks, keys, wide = weights_ref.shape
    kv_t_ref[...] = x_ref[:, :cells].reshape(keys, PAIR).T

    def chunk(t, carry):
        lanes = pl.ds(pl.multiple_of(t * wide, wide), wide)
        here = pl.ds(t * (wide // cells), wide // cells)
        queries_t = x_ref[here, cells:].reshape(wide, PAIR).T[:HEAD_DIM]
        queries = jnp.concatenate([queries_t, jnp.zeros((HEAD_DIM, wide), BF16)], axis=0)
        highest = jnp.full((8, wide), -jnp.inf, F32)
        for block in range(0, sectors, 2):
            rows = slice(block * cells, (block + 2) * cells)
            s = dot(x_ref[block : block + 2, :cells].reshape(2 * cells, PAIR), queries)
            s = s.reshape(2, cells, wide) + bias_ref[block : block + 2, lanes].reshape(2, 1, wide)
            s = s.reshape(2 * cells, wide)
            scores[rows, :] = s
            highest = jnp.maximum(highest, fold_rows(s, jnp.max))
        highest = jnp.max(highest, axis=0, keepdims=True)
        total = jnp.zeros((8, wide), F32)
        for block in range(0, sectors, 2):
            rows = slice(block * cells, (block + 2) * cells)
            p = jnp.exp2((scores[rows, :] - highest) * (SCALE * LOG2E))
            total = total + fold_rows(p, jnp.sum)
            weights_ref[t, rows, :] = p.astype(BF16)
        highest_ref[t] = highest
        total_ref[t] = jnp.sum(total, axis=0, keepdims=True)
        out_ref[t] = dot(kv_t_ref[HEAD_DIM:, :], weights_ref[t])
        return carry

    lax.fori_loop(0, chunks, chunk, 0)


def rims_kernel(
    x_ref, bias_ref, low_ref, high_ref, highest_ref, total_ref, out_ref,
    attended_ref, cot_ref, spread_ref, query_ref, low_grad_ref, high_grad_ref,
):
    sectors, both, _ = x_ref.shape
    cells = both // 2
    chunks, _, wide = out_ref.shape
    count = wide // cells
    parts = [slice(a * cells, (a + 1) * cells) for a in range(count)]

    def chunk(t, carry):
        lanes = pl.ds(pl.multiple_of(t * wide, wide), wide)
        first = t * count
        qc_t = x_ref[pl.ds(first, count), cells:].reshape(wide, PAIR).T
        zeros = jnp.zeros((HEAD_DIM, wide), BF16)
        queries = jnp.concatenate([qc_t[:HEAD_DIM], zeros], axis=0)
        rims = [
            jnp.concatenate([low_ref[first + a], high_ref[first + a]], axis=0)
            for a in range(count)
        ]
        rims_t = [rim.T for rim in rims]

        def beside(values):
            return jnp.concatenate(values, axis=1)

        s = beside([dot(rim, queries[:, part]) for rim, part in zip(rims, parts)])
        s = s.reshape(2, cells, wide) + bias_ref[sectors : sectors + 2, lanes].reshape(2, 1, wide)
        s = s.reshape(2 * cells, wide)
        own = highest_ref[t]
        highest = jnp.maximum(own, jnp.max(fold_rows(s, jnp.max), axis=0, keepdims=True))
        p = jnp.exp2((s - highest) * (SCALE * LOG2E))
        p_low = p.astype(BF16)
        ratio = jnp.exp2((own - highest) * (SCALE * LOG2E))
        total = ratio * total_ref[t] + jnp.sum(fold_rows(p, jnp.sum), axis=0, keepdims=True)
        inverse = 1.0 / total
        rim_out = [dot(rim_t[HEAD_DIM:], p_low[:, part]) for rim_t, part in zip(rims_t, parts)]
        out_t = out_ref[t] * ratio + beside(rim_out)
        attended = (out_t * inverse).astype(BF16)
        attended_ref[t] = attended
        cot_t = qc_t[HEAD_DIM:].astype(F32) * inverse
        own_cot = (cot_t * ratio).astype(BF16)
        cot_ref[t] = own_cot
        spread_ref[t] = jnp.sum(own_cot.astype(F32) * attended.astype(F32), axis=0, keepdims=True)
        cot_t = cot_t.astype(BF16)
        spread = jnp.sum(cot_t.astype(F32) * attended.astype(F32), axis=0, keepdims=True)
        cots = jnp.concatenate([zeros, cot_t], axis=0)
        product = beside([dot(rim, cots[:, part]) for rim, part in zip(rims, parts)])
        slopes = (p * (product - spread)).astype(BF16)
        query_ref[t] = beside(
            [dot(rim_t[:HEAD_DIM], slopes[:, part]) for rim_t, part in zip(rims_t, parts)]
        )
        for a, part in enumerate(parts):
            left = beside([p_low[:, part], slopes[:, part]])
            right = beside([cots[:, part], queries[:, part]])
            grad = dot(left, right, NT) * lane_scale()
            low_grad_ref[first + a] = grad[:cells].astype(BF16)
            high_grad_ref[first + a] = grad[cells:].astype(BF16)
        return carry

    lax.fori_loop(0, chunks, chunk, 0)


def backward_kernel(
    x_ref, kv_t_ref, weights_ref, attended_ref, cot_ref, spread_ref, query_ref,
    out_ref, grad_ref, slopes_scr,
):
    sectors, both, _ = x_ref.shape
    cells = both // 2
    chunks, keys, wide = weights_ref.shape
    grad_ref[...] = jnp.zeros_like(grad_ref)

    def chunk(t, carry):
        here = pl.ds(t * (wide // cells), wide // cells)
        queries_t = x_ref[here, cells:].reshape(wide, PAIR).T[:HEAD_DIM]
        zeros = jnp.zeros((HEAD_DIM, wide), BF16)
        queries = jnp.concatenate([queries_t, zeros], axis=0)
        cots = jnp.concatenate([zeros, cot_ref[t]], axis=0)
        spread = spread_ref[t]
        for block in range(0, sectors, 2):
            rows = slice(block * cells, (block + 2) * cells)
            product = dot(x_ref[block : block + 2, :cells].reshape(2 * cells, PAIR), cots)
            slopes = weights_ref[t, rows, :].astype(F32) * (product - spread)
            slopes_scr[rows, :] = slopes.astype(BF16)
        query_t = query_ref[t] + dot(kv_t_ref[:HEAD_DIM, :], slopes_scr[...])
        left = jnp.concatenate([weights_ref[t], slopes_scr[...]], axis=1)
        grad = dot(left, jnp.concatenate([cots, queries], axis=1), NT)
        grad_ref[...] += grad.reshape(sectors, cells, PAIR)
        packed = jnp.concatenate([(query_t * SCALE).astype(BF16), attended_ref[t]], axis=0)
        out_ref[here] = packed.T.reshape(wide // cells, cells, PAIR)
        return carry

    lax.fori_loop(0, chunks, chunk, 0)
    grad_ref[...] = grad_ref[...] * lane_scale().reshape(1, 1, PAIR)


def merge_kernel(out_ref, grad_ref, from_low_ref, from_high_ref, merged_ref):
    cells = out_ref.shape[1]
    merged_ref[:, :cells] = out_ref[...]
    grad = grad_ref[...] + from_low_ref[...].astype(F32) + from_high_ref[...].astype(F32)
    merged_ref[:, cells:] = grad.astype(BF16)


def unpack_kernel(merged_ref, attended_ref, query_ref, key_ref, value_ref):
    cells = attended_ref.shape[0]
    for head in range(0, HEADS, 2):
        lanes = slice(head * HEAD_DIM, (head + 2) * HEAD_DIM)
        for rows, first_ref, second_ref in (
            (slice(0, cells), query_ref, attended_ref),
            (slice(cells, 2 * cells), key_ref, value_ref),
        ):
            one, two = merged_ref[head, rows], merged_ref[head + 1, rows]
            first_ref[:, lanes] = jnp.concatenate([one[:, :HEAD_DIM], two[:, :HEAD_DIM]], axis=1)
            second_ref[:, lanes] = jnp.concatenate([one[:, HEAD_DIM:], two[:, HEAD_DIM:]], axis=1)


def cost(flops, nbytes):
    return pl.CostEstimate(flops=flops, bytes_accessed=nbytes, transcendentals=0)


def per_device(queries, key_vectors, value_vectors, cotangent, neighbour_lists, list_counts):
    _, band_rows, cycle_cols, features = queries.shape
    cells = band_rows * cycle_cols
    sectors = lax.axis_size("lon")
    bands = lax.axis_size("lat")
    chunks = sectors // CHUNK
    wide = CHUNK * cells
    keys = sectors * cells
    flat = (cells, features)
    params = pltpu.CompilerParams(vmem_limit_bytes=32 * 1024 * 1024)
    small = pltpu.CompilerParams(vmem_limit_bytes=16 * 1024 * 1024)
    struct = jax.ShapeDtypeStruct
    paired = struct((sectors, cells, PAIR), BF16)

    packed, bias = pl.pallas_call(
        pack_kernel,
        out_shape=(struct((HEADS, 2 * cells, PAIR), BF16), struct((sectors + 2, keys), F32)),
        in_specs=[SMEM] * 2 + [VMEM] * 4, out_specs=(VMEM,) * 2,
        cost_estimate=cost(0, 2 << 20), name="pack",
    )(
        neighbour_lists, list_counts, key_vectors.reshape(flat), value_vectors.reshape(flat),
        queries.reshape(flat), cotangent.reshape(flat),
    )
    x = lax.all_to_all(packed, "lon", 0, 0, tiled=True)
    kv = x[:, :cells]
    up = [(band, (band + 1) % bands) for band in range(bands)]
    down = [(target, source) for source, target in up]
    low = lax.ppermute(kv, "lat", up)
    high = lax.ppermute(kv, "lat", down)

    row_shape = struct((chunks, 1, wide), F32)
    tall_shape = struct((chunks, HEAD_DIM, wide), F32)
    tall_low = struct((chunks, HEAD_DIM, wide), BF16)

    weights, highest, total, out_t, kv_t = pl.pallas_call(
        forward_kernel,
        out_shape=(
            struct((chunks, keys, wide), BF16), row_shape, row_shape, tall_shape,
            struct((PAIR, keys), BF16),
        ),
        in_specs=[VMEM] * 2, out_specs=(VMEM,) * 5,
        scratch_shapes=[pltpu.VMEM((keys, wide), F32)],
        compiler_params=params, cost_estimate=cost(10**10, 10 << 20), name="forward",
    )(x, bias)
    attended, cot, spread, query_t, low_grad, high_grad = pl.pallas_call(
        rims_kernel,
        out_shape=(tall_low, tall_low, row_shape, tall_shape, paired, paired),
        in_specs=[VMEM] * 7, out_specs=(VMEM,) * 6,
        compiler_params=params, cost_estimate=cost(4 * 10**9, 4 << 20), name="rims",
    )(x, bias, low, high, highest, total, out_t)
    from_high = lax.ppermute(low_grad, "lat", down)
    from_low = lax.ppermute(high_grad, "lat", up)
    out, grad = pl.pallas_call(
        backward_kernel,
        out_shape=(paired, struct(paired.shape, F32)),
        in_specs=[VMEM] * 7, out_specs=(VMEM,) * 2,
        scratch_shapes=[pltpu.VMEM((keys, wide), BF16)],
        compiler_params=params, cost_estimate=cost(15 * 10**9, 12 << 20), name="backward",
    )(x, kv_t, weights, attended, cot, spread, query_t)
    merged = pl.pallas_call(
        merge_kernel, out_shape=struct((sectors, 2 * cells, PAIR), BF16),
        in_specs=[VMEM] * 4, out_specs=VMEM, compiler_params=small, cost_estimate=cost(0, 4 << 20), name="merge",
    )(out, grad, from_low, from_high)
    merged = lax.all_to_all(merged, "lon", 0, 0, tiled=True)
    results = pl.pallas_call(
        unpack_kernel, out_shape=(struct(flat, BF16),) * 4, in_specs=[VMEM], out_specs=(VMEM,) * 4,
        compiler_params=small, cost_estimate=cost(0, 2 << 20), name="unpack",
    )(merged)
    return tuple(result.reshape(queries.shape) for result in results)


def solution(mesh):
    blocks = P(None, "lat", "lon", None)
    return jax.shard_map(
        per_device, mesh=mesh, in_specs=(blocks,) * 4 + (P(), P()), out_specs=(blocks,) * 4,
        check_vma=False,
    )
```

time: 96.5 us -> 90 us (0.933)
  Pallas kernels: 37 us -> 25.3 us
  waiting for transfers between devices: 1.21 us -> 4.97 us
  blocking collectives: 49.7 us -> 51.2 us
    pallas_call x5, Pallas kernels: 35.6 us -> 24 us  [the longest x1 8.81 us: per_device(): pl.pallas_call(backward_kernel, out_shape=(paired, struct(paired.shape, F...]
    ppermute x1, waiting for transfers between devices: 1.21 us -> 4.03 us  [per_device(): low = lax.ppermute(kv, 'lat', up)]
    all_to_all x1, blocking collectives: 23.7 us -> 25.1 us  [per_device(): merged = lax.all_to_all(merged, 'lon', 0, 0, tiled=True)]
  transfers between devices with their start and end apart: 4 -> 4, of which waited for: 1 -> 3; matrix products, arithmetic and copies ran while one was open for 0% -> 0% of each run, Pallas kernels for 28% -> 19%
where the time goes in v2:
time: 90 us; the launch traced here: 89.8 us
  blocking collectives  51.2 us (57%)
  Pallas kernels  25.3 us (28%)
  starting transfers between devices  6.64 us (7%)
  waiting for transfers between devices  4.97 us (6%)
  local copies, waits for them, and re-layouts  0.97 us (1%)
    all_to_all x1, blocking collectives, per_device(): x = lax.all_to_all(packed, 'lon', 0, 0, tiled=True)  26 us
    all_to_all x1, blocking collectives, per_device(): merged = lax.all_to_all(merged, 'lon', 0, 0, tiled=True)  25.1 us
    pallas_call x1, Pallas kernels, per_device(): pl.pallas_call(backward_kernel, out_shape=(paired, struct(paired.shape, F...  8.81 us
    pallas_call x1, Pallas kernels, per_device(): pl.pallas_call(forward_kernel, out_shape=(struct((chunks, keys, wide), BF...  8.61 us
    ppermute x1, waiting for transfers between devices, per_device(): low = lax.ppermute(kv, 'lat', up)  4.03 us
    pallas_call x1, Pallas kernels, per_device(): pl.pallas_call(rims_kernel, out_shape=(tall_low, tall_low, row_shape, tal...  3.75 us
    ppermute x1, starting transfers between devices, per_device(): from_high = lax.ppermute(low_grad, 'lat', down)  3.56 us
    ppermute x1, starting transfers between devices, per_device(): high = lax.ppermute(kv, 'lat', down)  3 us
  transfers between devices with their start and end apart: 4, of which 3 were waited for; matrix products, arithmetic and copies ran while one was open for 0% of the time, Pallas kernels for 19%

profile of v2, /device:TPU:1, one launch (start us, length us, event | category | flops | bytes accessed | tf_op | source)
XLA Modules:
  0.0 89.8 jit_solution(17517411176774443596)
XLA Ops:
  0.6 2.6 %pack.1 = (bf16[16,256,128]{2,1,0:T(8,128)(2,1)}, f32[18,2048]{1,0:T(8,128)}) custom-call(s32[8,16]{1,0:T(8,128)} %lists_ref.1, s32[8]{0:T(128)} %counts_ref.1, bf16[128,1024]{1,0:T(8,128)(2,1)} %bitcast.8, bf16[128,1024]{1,0:T(8,128)(2,1)} %bitcast.9, bf16[128,1024]{1,0:T(8,128)(2,1)} %bitcast.10, bf16[128,1024]{1,0:T(8,128)(2,1)} %bitcast.11), custom_call_target="tpu_custom_call" | custom-call | bytes 2097152 | tf_op jit(solution)/shard_map/pack/pallas_call | solution.py:235
  3.3 26.0 %all_to_all.10.x_ref = bf16[16,256,128]{2,1,0:T(8,128)(2,1)S(1)} all-to-all(bf16[16,256,128]{2,1,0:T(8,128)(2,1)} %get-tuple-element.23), channel_id=1, replica_groups=mesh['lat'=8,'lon'=16] {'lon'}, dimensions={0} | all-to-all | bytes 2097152 | tf_op jit(solution)/shard_map/all_to_all | solution.py:244
  29.4 3.0 %collective-permute-start.1 = (bf16[16,128,128]{2,1,0:T(8,128)(2,1)S(1)}, bf16[16,128,128]{2,1,0:T(8,128)(2,1)S(1)}, u32[]{:S(2)}, u32[]{:S(2)}) collective-permute-start(bf16[16,128,128]{2,1,0:T(8,128)(2,1)S(1)} %slice.4), channel_id=1, source_target_pairs={{16,0},{32,16},{48,32},{64,48},{80,64},{96,80},{112,96},{0,112},{1... | collective-permute-start | bytes 1572872 | tf_op jit(solution)/shard_map/ppermute | solution.py:249
  32.4 0.0 collective-permute-start
  32.4 0.0 copy-start
  32.4 0.9 %copy-done = f32[18,2048]{1,0:T(8,128)S(1)} copy-done((f32[18,2048]{1,0:T(8,128)S(1)}, f32[18,2048]{1,0:T(8,128)}, u32[]{:S(2)}) %copy-start) | copy-done | bytes 147480
  33.3 8.6 %forward.1 = (bf16[4,2048,512]{2,1,0:T(8,128)(2,1)S(1)}, f32[4,1,512]{2,1,0:T(1,128)S(1)}, f32[4,1,512]{2,1,0:T(1,128)S(1)}, f32[4,64,512]{2,1,0:T(8,128)S(1)}, bf16[128,2048]{1,0:T(8,128)(2,1)S(1)}) custom-call(bf16[16,256,128]{2,1,0:T(8,128)(2,1)S(1)} %all_to_all.10.x_ref, f32[18,2048]{1,0:T(8,128)S(1)} %copy-done), custom_call_target="tpu_custom_call" | custom-call | flops 10000000000 | bytes 10485760 | tf_op jit(solution)/shard_map/forward/pallas_call | solution.py:255
  41.9 0.3 collective-permute-done.1.high_ref
  42.2 4.0 %collective-permute-done.low_ref = bf16[16,128,128]{2,1,0:T(8,128)(2,1)S(1)} collective-permute-done((bf16[16,128,128]{2,1,0:T(8,128)(2,1)S(1)}, bf16[16,128,128]{2,1,0:T(8,128)(2,1)S(1)}, u32[]{:S(2)}, u32[]{:S(2)}) %collective-permute-start) | collective-permute-done | bytes 524320 | tf_op jit(solution)/shard_map/ppermute | solution.py:248
  46.3 3.8 %rims.1 = (bf16[4,64,512]{2,1,0:T(8,128)(2,1)S(1)}, bf16[4,64,512]{2,1,0:T(8,128)(2,1)S(1)}, f32[4,1,512]{2,1,0:T(1,128)S(1)}, f32[4,64,512]{2,1,0:T(8,128)S(1)}...) custom-call(bf16[16,256,128]{2,1,0:T(8,128)(2,1)S(1)} %all_to_all.10.x_ref, ...), custom_call_target="tpu_custom_call" | custom-call | flops 4000000000 | bytes 4194304 | tf_op jit(solution)/shard_map/rims/pallas_call | solution.py:265
  50.0 0.1 collective-permute-start.2
  50.1 3.6 %collective-permute-start.3 = (bf16[16,128,128]{2,1,0:T(8,128)(2,1)S(1)}, bf16[16,128,128]{2,1,0:T(8,128)(2,1)S(1)}, u32[]{:S(2)}, u32[]{:S(2)}) collective-permute-start(bf16[16,128,128]{2,1,0:T(8,128)(2,1)S(1)} %get-tuple-element.37), channel_id=1, source_target_pairs={{16,0},{32,16},{48,32},{64,48},{80,64},{96,80},{112,96},{0,112},{1... | collective-permute-start | bytes 1572872 | tf_op jit(solution)/shard_map/ppermute | solution.py:271
  53.7 8.8 %backward.1 = (bf16[16,128,128]{2,1,0:T(8,128)(2,1)S(1)}, f32[16,128,128]{2,1,0:T(8,128)S(1)}) custom-call(bf16[16,256,128]{2,1,0:T(8,128)(2,1)S(1)} %all_to_all.10.x_ref, bf16[128,2048]{1,0:T(8,128)(2,1)S(1)} %get-tuple-element.25.kv_t_ref, bf16[4,2048,512]{2,1,0:T(8,128)(2,1)S(1)} %get-tuple-element.26.weights_ref, ...), custom_call_target="tpu_custom_call" | custom-call | flops 15000000512 | bytes 12582912 | tf_op jit(solution)/shard_map/backward/pallas_call | solution.py:273
  62.5 0.6 collective-permute-done.2.from_low_ref
  63.1 0.0 collective-permute-done.3.from_high_ref
  63.1 0.2 merge.1
  63.3 25.1 %all_to_all.11.merged_ref = bf16[16,256,128]{2,1,0:T(8,128)(2,1)S(1)} all-to-all(bf16[16,256,128]{2,1,0:T(8,128)(2,1)S(1)} %merge.1), channel_id=1, replica_groups=mesh['lat'=8,'lon'=16] {'lon'}, dimensions={0} | all-to-all | bytes 2097152 | tf_op jit(solution)/shard_map/all_to_all | solution.py:284
  88.5 1.3 %unpack.1 = (bf16[128,1024]{1,0:T(8,128)(2,1)}, bf16[128,1024]{1,0:T(8,128)(2,1)}, bf16[128,1024]{1,0:T(8,128)(2,1)}, bf16[128,1024]{1,0:T(8,128)(2,1)}) custom-call(bf16[16,256,128]{2,1,0:T(8,128)(2,1)S(1)} %all_to_all.11.merged_ref), custom_call_target="tpu_custom_call" | custom-call | bytes 2097152 | tf_op jit(solution)/shard_map/unpack/pallas_call | solution.py:285
  (1 shorter events, 0.0 us)
Async XLA Ops:
  29.4 12.9 %collective-permute-start.1 = (bf16[16,128,128]{2,1,0:T(8,128)(2,1)S(1)}, bf16[16,128,128]{2,1,0:T(8,128)(2,1)S(1)}, u32[]{:S(2)}, u32[]{:S(2)}) collective-permute-start(bf16[16,128,128]{2,1,0:T(8,128)(2,1)S(1)} %slice.4), channel_id=1, source_target_pairs={{16,0},{32,16},{48,32},{64,48},{80,64},{96,80},{112,96},{0,112},{1... | collective-permute-start | bytes 1572872 | tf_op jit(solution)/shard_map/ppermute | solution.py:249
  32.4 13.9 %collective-permute-start = (bf16[16,128,128]{2,1,0:T(8,128)(2,1)S(1)}, bf16[16,128,128]{2,1,0:T(8,128)(2,1)S(1)}, u32[]{:S(2)}, u32[]{:S(2)}) collective-permute-start(bf16[16,128,128]{2,1,0:T(8,128)(2,1)S(1)} %slice.4), channel_id=1, source_target_pairs={{0,16},{16,32},{32,48},{48,64},{64,80},{80,96},{96,112},{112,0},{1... | collective-permute-start | bytes 1572872 | tf_op jit(solution)/shard_map/ppermute | solution.py:248
  32.4 0.9 %copy-start = (f32[18,2048]{1,0:T(8,128)S(1)}, f32[18,2048]{1,0:T(8,128)}, u32[]{:S(2)}) copy-start(f32[18,2048]{1,0:T(8,128)} %get-tuple-element.24.bias_ref) | copy-start | bytes 442372
  50.0 13.1 %collective-permute-start.2 = (bf16[16,128,128]{2,1,0:T(8,128)(2,1)S(1)}, bf16[16,128,128]{2,1,0:T(8,128)(2,1)S(1)}, u32[]{:S(2)}, u32[]{:S(2)}) collective-permute-start(bf16[16,128,128]{2,1,0:T(8,128)(2,1)S(1)} %get-tuple-element.36), channel_id=1, source_target_pairs={{0,16},{16,32},{32,48},{48,64},{64,80},{80,96},{96,112},{112,0},{1... | collective-permute-start | bytes 1572872 | tf_op jit(solution)/shard_map/ppermute | solution.py:272
  50.1 13.0 %collective-permute-start.3 = (bf16[16,128,128]{2,1,0:T(8,128)(2,1)S(1)}, bf16[16,128,128]{2,1,0:T(8,128)(2,1)S(1)}, u32[]{:S(2)}, u32[]{:S(2)}) collective-permute-start(bf16[16,128,128]{2,1,0:T(8,128)(2,1)S(1)} %get-tuple-element.37), channel_id=1, source_target_pairs={{16,0},{32,16},{48,32},{64,48},{80,64},{96,80},{112,96},{0,112},{1... | collective-permute-start | bytes 1572872 | tf_op jit(solution)/shard_map/ppermute | solution.py:271

commit v3 on v2

v3 whole, which is shorter than its diff:
```python
import functools

import jax
import jax.numpy as jnp
from jax import lax
from jax.experimental import pallas as pl
from jax.experimental.pallas import tpu as pltpu
from jax.sharding import PartitionSpec as P

HEADS = 16
HEAD_DIM = 64
PAIR = 2 * HEAD_DIM
SCALE = HEAD_DIM ** (-0.5)
LOG2E = 1.4426950408889634
MASKED = -1e30
CHUNK = 4
BF16 = jnp.bfloat16
F32 = jnp.float32
NN = (((1,), (0,)), ((), ()))
NT = (((1,), (1,)), ((), ()))
VMEM = pl.BlockSpec(memory_space=pltpu.VMEM)
SMEM = pl.BlockSpec(memory_space=pltpu.SMEM)


def dot(a, b, dims=NN):
    return lax.dot_general(a, b, dims, preferred_element_type=F32)


def pack_pairs(first_ref, second_ref, out_ref, rows):
    for head in range(HEADS):
        lanes = slice(head * HEAD_DIM, (head + 1) * HEAD_DIM)
        out_ref[head, rows] = jnp.concatenate([first_ref[:, lanes], second_ref[:, lanes]], axis=1)


def pack_kernel(
    lists_ref, counts_ref, key_ref, value_ref, query_ref, cot_ref, packed_ref, bias_ref
):
    cells = key_ref.shape[0]
    pack_pairs(key_ref, value_ref, packed_ref, slice(0, cells))
    pack_pairs(query_ref, cot_ref, packed_ref, slice(cells, 2 * cells))
    band = lax.axis_index("lat")
    bands, slots = lists_ref.shape
    sectors = bias_ref.shape[0] - 2
    shape = (sectors, bias_ref.shape[1])
    key_sector = lax.broadcasted_iota(jnp.int32, shape, 0)
    query_sector = lax.broadcasted_iota(jnp.int32, shape, 1) // cells
    offset = key_sector - query_sector
    offset = jnp.where(offset < 0, offset + sectors, offset)
    count = counts_ref[band]
    bias = jnp.full(shape, MASKED, F32)
    for slot in range(slots):
        named = jnp.where(slot < count, lists_ref[band, slot], -1)
        bias = jnp.where(offset == named, 0.0, bias)
    bias_ref[:sectors] = bias
    outer = jnp.where((band > 0) & (band < bands - 1), 0.0, MASKED).astype(F32)
    row = lax.broadcasted_iota(jnp.int32, (2, shape[1]), 0)
    bias_ref[sectors:] = jnp.where(row == 0, 0.0, outer)


def lane_scale():
    lane = lax.broadcasted_iota(jnp.int32, (1, PAIR), 1)
    return jnp.where(lane < HEAD_DIM, SCALE, 1.0).astype(F32)


def fold_rows(values, combine):
    return combine(values.reshape(values.shape[0] // 8, 8, values.shape[1]), axis=0)


def forward_part(start, x_ref, bias_ref, kv_t_ref, weights_ref, highest_ref, total_ref, out_ref, scores):
    sectors, both, _ = x_ref.shape
    cells = both // 2
    chunks, keys, wide = weights_ref.shape
    count = wide // cells
    blocks = [slice(block * cells, (block + 2) * cells) for block in range(0, sectors, 2)]

    def score(t, queries, rows, highest):
        block = rows.start // cells
        lanes = slice((start + t) * wide, (start + t + 1) * wide)
        s = dot(x_ref[block : block + 2, :cells].reshape(2 * cells, PAIR), queries, NT)
        s = s.reshape(2, cells, wide) + bias_ref[block : block + 2, lanes].reshape(2, 1, wide)
        s = s.reshape(2 * cells, wide)
        scores[t, rows, :] = s
        return jnp.maximum(highest, fold_rows(s, jnp.max))

    lane = lax.broadcasted_iota(jnp.int32, (1, PAIR), 1)
    highest = total = None
    for t in range(chunks + 1):
        before, before_highest = t - 1, highest
        if t < chunks:
            qc = x_ref[(start + t) * count : (start + t + 1) * count, cells:].reshape(wide, PAIR)
            queries = jnp.where(lane < HEAD_DIM, qc, jnp.zeros_like(qc))
            highest = jnp.full((8, wide), -jnp.inf, F32)
        total = jnp.zeros((8, wide), F32)
        for rows in blocks:
            if t < chunks:
                highest = score(t, queries, rows, highest)
            if t > 0:
                p = jnp.exp2((scores[before, rows, :] - before_highest) * (SCALE * LOG2E))
                total = total + fold_rows(p, jnp.sum)
                weights_ref[before, rows, :] = p.astype(BF16)
        if t > 0:
            highest_ref[before] = before_highest
            total_ref[before] = jnp.sum(total, axis=0, keepdims=True)
            out_ref[before] = dot(kv_t_ref[HEAD_DIM:, :], weights_ref[before])
        highest = jnp.max(highest, axis=0, keepdims=True)


def first_forward_kernel(x_ref, bias_ref, *refs):
    *outs, kv_t_ref, kv_ref, scores = refs
    cells = kv_ref.shape[1]
    kv_ref[...] = x_ref[kv_ref.shape[0] :, :cells]
    kv_t_ref[...] = x_ref[:, :cells].reshape(kv_t_ref.shape[1], PAIR).T
    forward_part(0, x_ref, bias_ref, kv_t_ref, *outs, scores)


def rims_kernel(
    start, x_ref, bias_ref, near_ref, far_ref, highest_ref, total_ref, out_ref, _,
    attended_ref, cot_ref, spread_ref, query_ref, near_grad_ref, far_grad_ref,
):
    sectors, both, _ = x_ref.shape
    cells = both // 2
    chunks, _, wide = out_ref.shape
    count = wide // cells
    parts = [slice(a * cells, (a + 1) * cells) for a in range(count)]

    def chunk(t, carry):
        lanes = pl.ds(pl.multiple_of((start + t) * wide, wide), wide)
        first = t * count
        qc_t = x_ref[pl.ds(start * count + first, count), cells:].reshape(wide, PAIR).T
        zeros = jnp.zeros((HEAD_DIM, wide), BF16)
        queries = jnp.concatenate([qc_t[:HEAD_DIM], zeros], axis=0)
        rims = [
            jnp.concatenate([near_ref[first + a], far_ref[first + a]], axis=0)
            for a in range(count)
        ]
        rims_t = [rim.T for rim in rims]

        def beside(values):
            return jnp.concatenate(values, axis=1)

        s = beside([dot(rim, queries[:, part]) for rim, part in zip(rims, parts)])
        s = s.reshape(2, cells, wide) + bias_ref[sectors : sectors + 2, lanes].reshape(2, 1, wide)
        s = s.reshape(2 * cells, wide)
        own = highest_ref[t]
        highest = jnp.maximum(own, jnp.max(fold_rows(s, jnp.max), axis=0, keepdims=True))
        p = jnp.exp2((s - highest) * (SCALE * LOG2E))
        p_low = p.astype(BF16)
        ratio = jnp.exp2((own - highest) * (SCALE * LOG2E))
        total = ratio * total_ref[t] + jnp.sum(fold_rows(p, jnp.sum), axis=0, keepdims=True)
        inverse = 1.0 / total
        rim_out = [dot(rim_t[HEAD_DIM:], p_low[:, part]) for rim_t, part in zip(rims_t, parts)]
        out_t = out_ref[t] * ratio + beside(rim_out)
        attended = (out_t * inverse).astype(BF16)
        attended_ref[t] = attended
        cot_t = qc_t[HEAD_DIM:].astype(F32) * inverse
        own_cot = (cot_t * ratio).astype(BF16)
        cot_ref[t] = own_cot
        spread_ref[t] = jnp.sum(own_cot.astype(F32) * attended.astype(F32), axis=0, keepdims=True)
        cot_t = cot_t.astype(BF16)
        spread = jnp.sum(cot_t.astype(F32) * attended.astype(F32), axis=0, keepdims=True)
        cots = jnp.concatenate([zeros, cot_t], axis=0)
        product = beside([dot(rim, cots[:, part]) for rim, part in zip(rims, parts)])
        slopes = (p * (product - spread)).astype(BF16)
        query_ref[t] = beside(
            [dot(rim_t[:HEAD_DIM], slopes[:, part]) for rim_t, part in zip(rims_t, parts)]
        )
        for a, part in enumerate(parts):
            left = beside([p_low[:, part], slopes[:, part]])
            right = beside([cots[:, part], queries[:, part]])
            grad = dot(left, right, NT) * lane_scale()
            near_grad_ref[first + a] = grad[:cells].astype(BF16)
            far_grad_ref[first + a] = grad[cells:].astype(BF16)
        return carry

    lax.fori_loop(0, chunks, chunk, 0)


def backward_kernel(
    start, x_ref, kv_t_ref, weights_ref, attended_ref, cot_ref, spread_ref, query_ref, *refs
):
    *before, out_ref, grad_ref, slopes_scr = refs
    sectors, both, _ = x_ref.shape
    cells = both // 2
    chunks, keys, wide = weights_ref.shape
    grad_ref[...] = before[0][...] if before else jnp.zeros_like(grad_ref)

    def chunk(t, carry):
        count = wide // cells
        queries_t = x_ref[pl.ds((start + t) * count, count), cells:].reshape(wide, PAIR).T[:HEAD_DIM]
        zeros = jnp.zeros((HEAD_DIM, wide), BF16)
        queries = jnp.concatenate([queries_t, zeros], axis=0)
        cots = jnp.concatenate([zeros, cot_ref[t]], axis=0)
        spread = spread_ref[t]
        for block in range(0, sectors, 2):
            rows = slice(block * cells, (block + 2) * cells)
            product = dot(x_ref[block : block + 2, :cells].reshape(2 * cells, PAIR), cots)
            slopes = weights_ref[t, rows, :].astype(F32) * (product - spread)
            slopes_scr[rows, :] = slopes.astype(BF16)
        query_t = query_ref[t] + dot(kv_t_ref[:HEAD_DIM, :], slopes_scr[...])
        left = jnp.concatenate([weights_ref[t], slopes_scr[...]], axis=1)
        grad = dot(left, jnp.concatenate([cots, queries], axis=1), NT)
        grad_ref[...] += grad.reshape(sectors, cells, PAIR)
        packed = jnp.concatenate([(query_t * SCALE).astype(BF16), attended_ref[t]], axis=0)
        out_ref[pl.ds(t * count, count)] = packed.T.reshape(count, cells, PAIR)
        return carry

    lax.fori_loop(0, chunks, chunk, 0)


def merge_kernel(grad_ref, *refs):
    *part_refs, merged_ref = refs
    cells = grad_ref.shape[1]
    start = 0
    for out_ref, near_ref, far_ref in zip(part_refs[::3], part_refs[1::3], part_refs[2::3]):
        part = slice(start, start + out_ref.shape[0])
        merged_ref[part, :cells] = out_ref[...]
        grad = grad_ref[part] * lane_scale().reshape(1, 1, PAIR)
        grad = grad + near_ref[...].astype(F32) + far_ref[...].astype(F32)
        merged_ref[part, cells:] = grad.astype(BF16)
        start = part.stop


def unpack_kernel(merged_ref, attended_ref, query_ref, key_ref, value_ref):
    cells = attended_ref.shape[0]
    for head in range(0, HEADS, 2):
        lanes = slice(head * HEAD_DIM, (head + 2) * HEAD_DIM)
        for rows, first_ref, second_ref in (
            (slice(0, cells), query_ref, attended_ref),
            (slice(cells, 2 * cells), key_ref, value_ref),
        ):
            one, two = merged_ref[head, rows], merged_ref[head + 1, rows]
            first_ref[:, lanes] = jnp.concatenate([one[:, :HEAD_DIM], two[:, :HEAD_DIM]], axis=1)
            second_ref[:, lanes] = jnp.concatenate([one[:, HEAD_DIM:], two[:, HEAD_DIM:]], axis=1)


def cost(flops, nbytes):
    return pl.CostEstimate(flops=flops, bytes_accessed=nbytes, transcendentals=0)


def per_device(queries, key_vectors, value_vectors, cotangent, neighbour_lists, list_counts):
    _, band_rows, cycle_cols, features = queries.shape
    cells = band_rows * cycle_cols
    sectors = lax.axis_size("lon")
    bands = lax.axis_size("lat")
    part = sectors // 2
    steps = part // CHUNK
    wide = CHUNK * cells
    keys = sectors * cells
    flat = (cells, features)
    params = pltpu.CompilerParams(vmem_limit_bytes=24 * 1024 * 1024)
    struct = jax.ShapeDtypeStruct

    def both_ways(to_near, to_far):
        return lax.ppermute(to_near, "lat", near), lax.ppermute(to_far, "lat", far)

    def call(kernel, outs, args, name, flops, specs=None, scratch=(), compiler_params=params):
        return pl.pallas_call(
            kernel, out_shape=outs, in_specs=specs or [VMEM] * len(args),
            out_specs=(VMEM,) * len(outs), scratch_shapes=scratch,
            compiler_params=compiler_params, cost_estimate=cost(flops, 4 << 20), name=name,
        )(*args)

    packed, bias = call(
        pack_kernel,
        (struct((HEADS, 2 * cells, PAIR), BF16), struct((sectors + 2, keys), F32)),
        (neighbour_lists, list_counts)
        + tuple(a.reshape(flat) for a in (key_vectors, value_vectors, queries, cotangent)),
        "pack", 0, [SMEM] * 2 + [VMEM] * 4, compiler_params=None,
    )
    x = lax.all_to_all(packed, "lon", 0, 0, tiled=True)
    near = [(band, band ^ 1) for band in range(bands)]
    far = [(band, ((band + 1) ^ 1) - 1) for band in range(1, bands - 1)]
    far += [(0, bands - 1), (bands - 1, 0)]

    row = struct((steps, 1, wide), F32)
    tall = struct((steps, HEAD_DIM, wide), F32)
    tall_low = struct(tall.shape, BF16)
    by_part = struct((part, cells, PAIR), BF16)
    ahead = (struct((steps, keys, wide), BF16), row, row, tall)
    scores = [pltpu.VMEM((steps, keys, wide), F32)]

    kv = x[:part, :cells]
    rims = [both_ways(kv, kv)]
    weights, *stats, kv_t, kv = call(
        first_forward_kernel, ahead + (struct((PAIR, keys), BF16), by_part), (x, bias),
        "forward", 5 * 10**9, scratch=scores,
    )
    forward = [(weights, stats)]
    rims.append(both_ways(kv, kv))
    weights, *stats = call(
        functools.partial(forward_part, steps), ahead, (x, bias, kv_t), "forward", 5 * 10**9,
        scratch=scores,
    )
    forward.append((weights, stats))
    last = stats[0]
    before, returned = (), []
    for i, (weights, stats) in enumerate(forward):
        *for_queries, near_grad, far_grad = call(
            functools.partial(rims_kernel, i * steps),
            (tall_low, tall_low, row, tall, by_part, by_part),
            (x, bias) + rims[i] + tuple(stats) + (last,), "rims", 10**9,
        )
        from_rims = both_ways(near_grad, far_grad)
        out, grad = call(
            functools.partial(backward_kernel, i * steps),
            (by_part, struct((sectors, cells, PAIR), F32)),
            (x, kv_t, weights) + tuple(for_queries) + before, "backward", 5 * 10**9,
            scratch=[pltpu.VMEM((keys, wide), BF16)],
        )
        before, last = (grad,) + from_rims, out
        returned += [out, *from_rims]
    (merged,) = call(
        merge_kernel, (struct((sectors, 2 * cells, PAIR), BF16),), (grad, *returned), "merge", 0
    )
    merged = lax.all_to_all(merged, "lon", 0, 0, tiled=True)
    results = call(unpack_kernel, (struct(flat, BF16),) * 4, (merged,), "unpack", 0)
    return tuple(result.reshape(queries.shape) for result in results)


def solution(mesh):
    blocks = P(None, "lat", "lon", None)
    return jax.shard_map(
        per_device, mesh=mesh, in_specs=(blocks,) * 4 + (P(), P()), out_specs=(blocks,) * 4,
        check_vma=False,
    )
```

time: 90 us -> 87 us (0.967)
  waiting for transfers between devices: 4.97 us -> 1.61 us
  starting transfers between devices: 6.64 us -> 9.18 us
  Pallas kernels: 25.3 us -> 24.1 us
  blocking collectives: 51.2 us -> 50.1 us
    ppermute x4 -> x8, waiting for transfers between devices: 4.97 us -> 1.61 us  [the longest x4 1.6 us: both_ways(): lax.ppermute(to_far, 'lat', far)]
    ppermute x4 -> x8, starting transfers between devices: 6.64 us -> 9.18 us  [the longest x4 7.22 us: both_ways(): lax.ppermute(to_far, 'lat', far)]
    pallas_call x6 -> x9, Pallas kernels: 25.3 us -> 24.1 us  [call(): pl.pallas_call(kernel, out_shape=outs, in_specs=specs or [VMEM] * len(arg...]
    all_to_all x1, blocking collectives: 25.1 us -> 24.1 us  [per_device(): merged = lax.all_to_all(merged, 'lon', 0, 0, tiled=True)]
  transfers between devices with their start and end apart: 4 -> 8, of which waited for: 3 -> 1; matrix products, arithmetic and copies ran while one was open for 0% -> 0% of each run, Pallas kernels for 19% -> 23%
where the time goes in v3:
time: 87 us; the launch traced here: 86.7 us
  blocking collectives  50.1 us (58%)
  Pallas kernels  24.1 us (28%)
  starting transfers between devices  9.18 us (11%)
  waiting for transfers between devices  1.61 us (2%)
  local copies, waits for them, and re-layouts  0.94 us (1%)
    all_to_all x1, blocking collectives, per_device(): x = lax.all_to_all(packed, 'lon', 0, 0, tiled=True)  26 us
    pallas_call x9, Pallas kernels, call(): pl.pallas_call(kernel, out_shape=outs, in_specs=specs or [VMEM] * len(arg...  24.1 us
    all_to_all x1, blocking collectives, per_device(): merged = lax.all_to_all(merged, 'lon', 0, 0, tiled=True)  24.1 us
    ppermute x4, starting transfers between devices, both_ways(): lax.ppermute(to_far, 'lat', far)  7.22 us
    ppermute x4, starting transfers between devices, both_ways(): lax.ppermute(to_near, 'lat', near)  1.96 us
  transfers between devices with their start and end apart: 8, of which 1 were waited for; matrix products, arithmetic and copies ran while one was open for 0% of the time, Pallas kernels for 23%

profile of v3, /device:TPU:1, one launch (start us, length us, event | category | flops | bytes accessed | tf_op | source)
XLA Modules:
  0.0 86.7 jit_solution(8687934518317290354)
XLA Ops:
  0.6 2.6 %pack.1 = (bf16[16,256,128]{2,1,0:T(8,128)(2,1)}, f32[18,2048]{1,0:T(8,128)}) custom-call(s32[8,16]{1,0:T(8,128)} %lists_ref.1, s32[8]{0:T(128)} %counts_ref.1, bf16[128,1024]{1,0:T(8,128)(2,1)} %bitcast.8, bf16[128,1024]{1,0:T(8,128)(2,1)} %bitcast.9, bf16[128,1024]{1,0:T(8,128)(2,1)} %bitcast.10, bf16[128,1024]{1,0:T(8,128)(2,1)} %bitcast.11), custom_call_target="tpu_custom_call" | custom-call | bytes 4194304 | tf_op jit(solution)/shard_map/pack/pallas_call | solution.py:257
  3.3 26.0 %all_to_all.10.x_ref = bf16[16,256,128]{2,1,0:T(8,128)(2,1)S(1)} all-to-all(bf16[16,256,128]{2,1,0:T(8,128)(2,1)} %get-tuple-element.36), channel_id=1, replica_groups=mesh['lat'=8,'lon'=16] {'lon'}, dimensions={0} | all-to-all | bytes 2097152 | tf_op jit(solution)/shard_map/all_to_all | solution.py:270
  29.3 1.3 %collective-permute-start.2 = (bf16[8,128,128]{2,1,0:T(8,128)(2,1)S(1)}, bf16[8,128,128]{2,1,0:T(8,128)(2,1)S(1)}, u32[]{:S(2)}, u32[]{:S(2)}) collective-permute-start(bf16[8,128,128]{2,1,0:T(8,128)(2,1)S(1)} %slice.4), channel_id=1, source_target_pairs={{0,16},{16,0},{32,48},{48,32},{64,80},{80,64},{96,112},{112,96},{1... | collective-permute-start | bytes 786440 | tf_op jit(solution)/shard_map/ppermute | solution.py:254
  30.6 2.3 %collective-permute-start.3 = (bf16[8,128,128]{2,1,0:T(8,128)(2,1)S(1)}, bf16[8,128,128]{2,1,0:T(8,128)(2,1)S(1)}, u32[]{:S(2)}, u32[]{:S(2)}) collective-permute-start(bf16[8,128,128]{2,1,0:T(8,128)(2,1)S(1)} %slice.4), channel_id=1, source_target_pairs={{16,32},{32,16},{48,64},{64,48},{80,96},{96,80},{0,112},{112,0},{1... | collective-permute-start | bytes 786440 | tf_op jit(solution)/shard_map/ppermute | solution.py:254
  32.9 0.0 copy-start
  32.9 0.9 %copy-done = f32[18,2048]{1,0:T(8,128)S(1)} copy-done((f32[18,2048]{1,0:T(8,128)S(1)}, f32[18,2048]{1,0:T(8,128)}, u32[]{:S(2)}) %copy-start) | copy-done | bytes 147480
  33.8 3.7 %forward.2 = (bf16[2,2048,512]{2,1,0:T(8,128)(2,1)S(1)}, f32[2,1,512]{2,1,0:T(1,128)S(1)}, f32[2,1,512]{2,1,0:T(1,128)S(1)}, f32[2,64,512]{2,1,0:T(8,128)S(1)}, ...) custom-call(bf16[16,256,128]{2,1,0:T(8,128)(2,1)S(1)} %all_to_all.10.x_ref, f32[18,2048]{1,0:T(8,128)S(1)} %copy-done), custom_call_target="tpu_custom_call" | custom-call | flops 5000000000 | bytes 4194304 | tf_op jit(solution)/shard_map/forward/pallas_call | solution.py:257
  37.5 0.1 collective-permute-start
  37.6 1.4 %collective-permute-start.1 = (bf16[8,128,128]{2,1,0:T(8,128)(2,1)S(1)}, bf16[8,128,128]{2,1,0:T(8,128)(2,1)S(1)}, u32[]{:S(2)}, u32[]{:S(2)}) collective-permute-start(bf16[8,128,128]{2,1,0:T(8,128)(2,1)S(1)} %get-tuple-element.40), channel_id=1, source_target_pairs={{16,32},{32,16},{48,64},{64,48},{80,96},{96,80},{0,112},{112,0},{1... | collective-permute-start | bytes 786440 | tf_op jit(solution)/shard_map/ppermute | solution.py:254
  39.0 3.7 %forward.3 = (bf16[2,2048,512]{2,1,0:T(8,128)(2,1)S(1)}, f32[2,1,512]{2,1,0:T(1,128)S(1)}, f32[2,1,512]{2,1,0:T(1,128)S(1)}, f32[2,64,512]{2,1,0:T(8,128)S(1)}) custom-call(bf16[16,256,128]{2,1,0:T(8,128)(2,1)S(1)} %all_to_all.10.x_ref, f32[18,2048]{1,0:T(8,128)S(1)} %copy-done, bf16[128,2048]{1,0:T(8,128)(2,1)S(1)} %get-tuple-element.38.kv_t_ref), custom_call_target="tpu_custom_call" | custom-call | flops 5000000000 | bytes 4194304 | tf_op jit(solution)/shard_map/forward/pallas_call | solution.py:257
  42.7 0.0 collective-permute-done.2.near_ref
  42.7 0.0 collective-permute-done.3.far_ref
  42.7 1.9 %rims.2 = (bf16[2,64,512]{2,1,0:T(8,128)(2,1)S(1)}, bf16[2,64,512]{2,1,0:T(8,128)(2,1)S(1)}, f32[2,1,512]{2,1,0:T(1,128)S(1)}, f32[2,64,512]{2,1,0:T(8,128)S(1)}...) custom-call(bf16[16,256,128]{2,1,0:T(8,128)(2,1)S(1)} %all_to_all.10.x_ref, f32[18,2048]{1,0:T(8,128)S(1)} %copy-done, ...), custom_call_target="tpu_custom_call" | custom-call | flops 1000000000 | bytes 4194304 | tf_op jit(solution)/shard_map/rims/pallas_call | solution.py:257
  44.6 0.4 collective-permute-start.4
  45.0 2.3 %collective-permute-start.5 = (bf16[8,128,128]{2,1,0:T(8,128)(2,1)S(1)}, bf16[8,128,128]{2,1,0:T(8,128)(2,1)S(1)}, u32[]{:S(2)}, u32[]{:S(2)}) collective-permute-start(bf16[8,128,128]{2,1,0:T(8,128)(2,1)S(1)} %get-tuple-element.59), channel_id=1, source_target_pairs={{16,32},{32,16},{48,64},{64,48},{80,96},{96,80},{0,112},{112,0},{1... | collective-permute-start | bytes 786440 | tf_op jit(solution)/shard_map/ppermute | solution.py:254
  47.3 4.4 %backward.2 = (bf16[8,128,128]{2,1,0:T(8,128)(2,1)S(1)}, f32[16,128,128]{2,1,0:T(8,128)S(1)}) custom-call(bf16[16,256,128]{2,1,0:T(8,128)(2,1)S(1)} %all_to_all.10.x_ref, bf16[128,2048]{1,0:T(8,128)(2,1)S(1)} %get-tuple-element.38.kv_t_ref, bf16[2,2048,512]{2,1,0:T(8,128)(2,1)S(1)} %get-tuple-element.44.weights_ref, ...), custom_call_target="tpu_custom_call" | custom-call | flops 5000000000 | bytes 4194304 | tf_op jit(solution)/shard_map/backward/pallas_call | solution.py:257
  51.7 0.0 collective-permute-done.near_ref
  51.7 0.0 collective-permute-done.1.far_ref
  51.7 1.9 %rims.3 = (bf16[2,64,512]{2,1,0:T(8,128)(2,1)S(1)}, bf16[2,64,512]{2,1,0:T(8,128)(2,1)S(1)}, f32[2,1,512]{2,1,0:T(1,128)S(1)}, f32[2,64,512]{2,1,0:T(8,128)S(1)}...) custom-call(bf16[16,256,128]{2,1,0:T(8,128)(2,1)S(1)} %all_to_all.10.x_ref, f32[18,2048]{1,0:T(8,128)S(1)} %copy-done, ...), custom_call_target="tpu_custom_call" | custom-call | flops 1000000000 | bytes 4194304 | tf_op jit(solution)/shard_map/rims/pallas_call | solution.py:257
  53.6 0.2 collective-permute-start.6
  53.8 1.3 %collective-permute-start.7 = (bf16[8,128,128]{2,1,0:T(8,128)(2,1)S(1)}, bf16[8,128,128]{2,1,0:T(8,128)(2,1)S(1)}, u32[]{:S(2)}, u32[]{:S(2)}) collective-permute-start(bf16[8,128,128]{2,1,0:T(8,128)(2,1)S(1)} %get-tuple-element.63), channel_id=1, source_target_pairs={{16,32},{32,16},{48,64},{64,48},{80,96},{96,80},{0,112},{112,0},{1... | collective-permute-start | bytes 786440 | tf_op jit(solution)/shard_map/ppermute | solution.py:254
  55.1 0.0 collective-permute-done.4.refs_1_
  55.1 0.0 collective-permute-done.5.refs_2_
  55.1 4.4 %backward.3 = (bf16[8,128,128]{2,1,0:T(8,128)(2,1)S(1)}, f32[16,128,128]{2,1,0:T(8,128)S(1)}) custom-call(bf16[16,256,128]{2,1,0:T(8,128)(2,1)S(1)} %all_to_all.10.x_ref, bf16[128,2048]{1,0:T(8,128)(2,1)S(1)} %get-tuple-element.38.kv_t_ref, bf16[2,2048,512]{2,1,0:T(8,128)(2,1)S(1)} %get-tuple-element.39.weights_ref, ...), custom_call_target="tpu_custom_call" | custom-call | flops 5000000000 | bytes 4194304 | tf_op jit(solution)/shard_map/backward/pallas_call | solution.py:257
  59.5 0.0 collective-permute-done.6.refs_4_
  59.5 1.6 %collective-permute-done.7.refs_5_ = bf16[8,128,128]{2,1,0:T(8,128)(2,1)S(1)} collective-permute-done((bf16[8,128,128]{2,1,0:T(8,128)(2,1)S(1)}, bf16[8,128,128]{2,1,0:T(8,128)(2,1)S(1)}, u32[]{:S(2)}, u32[]{:S(2)}) %collective-permute-start.7) | collective-permute-done | bytes 262176 | tf_op jit(solution)/shard_map/ppermute | solution.py:254
  61.1 0.2 merge.1
  61.3 24.1 %all_to_all.11.merged_ref = bf16[16,256,128]{2,1,0:T(8,128)(2,1)S(1)} all-to-all(bf16[16,256,128]{2,1,0:T(8,128)(2,1)S(1)} %merge.1), channel_id=1, replica_groups=mesh['lat'=8,'lon'=16] {'lon'}, dimensions={0} | all-to-all | bytes 2097152 | tf_op jit(solution)/shard_map/all_to_all | solution.py:315
  85.4 1.3 %unpack.1 = (bf16[128,1024]{1,0:T(8,128)(2,1)}, bf16[128,1024]{1,0:T(8,128)(2,1)}, bf16[128,1024]{1,0:T(8,128)(2,1)}, bf16[128,1024]{1,0:T(8,128)(2,1)}) custom-call(bf16[16,256,128]{2,1,0:T(8,128)(2,1)S(1)} %all_to_all.11.merged_ref), custom_call_target="tpu_custom_call" | custom-call | bytes 4194304 | tf_op jit(solution)/shard_map/unpack/pallas_call | solution.py:257
  (1 shorter events, 0.0 us)
Async XLA Ops:
  29.3 13.4 %collective-permute-start.2 = (bf16[8,128,128]{2,1,0:T(8,128)(2,1)S(1)}, bf16[8,128,128]{2,1,0:T(8,128)(2,1)S(1)}, u32[]{:S(2)}, u32[]{:S(2)}) collective-permute-start(bf16[8,128,128]{2,1,0:T(8,128)(2,1)S(1)} %slice.4), channel_id=1, source_target_pairs={{0,16},{16,0},{32,48},{48,32},{64,80},{80,64},{96,112},{112,96},{1... | collective-permute-start | bytes 786440 | tf_op jit(solution)/shard_map/ppermute | solution.py:254
  30.6 12.1 %collective-permute-start.3 = (bf16[8,128,128]{2,1,0:T(8,128)(2,1)S(1)}, bf16[8,128,128]{2,1,0:T(8,128)(2,1)S(1)}, u32[]{:S(2)}, u32[]{:S(2)}) collective-permute-start(bf16[8,128,128]{2,1,0:T(8,128)(2,1)S(1)} %slice.4), channel_id=1, source_target_pairs={{16,32},{32,16},{48,64},{64,48},{80,96},{96,80},{0,112},{112,0},{1... | collective-permute-start | bytes 786440 | tf_op jit(solution)/shard_map/ppermute | solution.py:254
  32.9 0.9 %copy-start = (f32[18,2048]{1,0:T(8,128)S(1)}, f32[18,2048]{1,0:T(8,128)}, u32[]{:S(2)}) copy-start(f32[18,2048]{1,0:T(8,128)} %get-tuple-element.37.bias_ref) | copy-start | bytes 442372
  37.5 14.2 %collective-permute-start = (bf16[8,128,128]{2,1,0:T(8,128)(2,1)S(1)}, bf16[8,128,128]{2,1,0:T(8,128)(2,1)S(1)}, u32[]{:S(2)}, u32[]{:S(2)}) collective-permute-start(bf16[8,128,128]{2,1,0:T(8,128)(2,1)S(1)} %get-tuple-element.40), channel_id=1, source_target_pairs={{0,16},{16,0},{32,48},{48,32},{64,80},{80,64},{96,112},{112,96},{1... | collective-permute-start | bytes 786440 | tf_op jit(solution)/shard_map/ppermute | solution.py:254
  37.6 14.1 %collective-permute-start.1 = (bf16[8,128,128]{2,1,0:T(8,128)(2,1)S(1)}, bf16[8,128,128]{2,1,0:T(8,128)(2,1)S(1)}, u32[]{:S(2)}, u32[]{:S(2)}) collective-permute-start(bf16[8,128,128]{2,1,0:T(8,128)(2,1)S(1)} %get-tuple-element.40), channel_id=1, source_target_pairs={{16,32},{32,16},{48,64},{64,48},{80,96},{96,80},{0,112},{112,0},{1... | collective-permute-start | bytes 786440 | tf_op jit(solution)/shard_map/ppermute | solution.py:254
  44.6 10.5 %collective-permute-start.4 = (bf16[8,128,128]{2,1,0:T(8,128)(2,1)S(1)}, bf16[8,128,128]{2,1,0:T(8,128)(2,1)S(1)}, u32[]{:S(2)}, u32[]{:S(2)}) collective-permute-start(bf16[8,128,128]{2,1,0:T(8,128)(2,1)S(1)} %get-tuple-element.58), channel_id=1, source_target_pairs={{0,16},{16,0},{32,48},{48,32},{64,80},{80,64},{96,112},{112,96},{1... | collective-permute-start | bytes 786440 | tf_op jit(solution)/shard_map/ppermute | solution.py:254
  45.0 10.1 %collective-permute-start.5 = (bf16[8,128,128]{2,1,0:T(8,128)(2,1)S(1)}, bf16[8,128,128]{2,1,0:T(8,128)(2,1)S(1)}, u32[]{:S(2)}, u32[]{:S(2)}) collective-permute-start(bf16[8,128,128]{2,1,0:T(8,128)(2,1)S(1)} %get-tuple-element.59), channel_id=1, source_target_pairs={{16,32},{32,16},{48,64},{64,48},{80,96},{96,80},{0,112},{112,0},{1... | collective-permute-start | bytes 786440 | tf_op jit(solution)/shard_map/ppermute | solution.py:254
  53.6 5.9 %collective-permute-start.6 = (bf16[8,128,128]{2,1,0:T(8,128)(2,1)S(1)}, bf16[8,128,128]{2,1,0:T(8,128)(2,1)S(1)}, u32[]{:S(2)}, u32[]{:S(2)}) collective-permute-start(bf16[8,128,128]{2,1,0:T(8,128)(2,1)S(1)} %get-tuple-element.62), channel_id=1, source_target_pairs={{0,16},{16,0},{32,48},{48,32},{64,80},{80,64},{96,112},{112,96},{1... | collective-permute-start | bytes 786440 | tf_op jit(solution)/shard_map/ppermute | solution.py:254
  53.8 7.3 %collective-permute-start.7 = (bf16[8,128,128]{2,1,0:T(8,128)(2,1)S(1)}, bf16[8,128,128]{2,1,0:T(8,128)(2,1)S(1)}, u32[]{:S(2)}, u32[]{:S(2)}) collective-permute-start(bf16[8,128,128]{2,1,0:T(8,128)(2,1)S(1)} %get-tuple-element.63), channel_id=1, source_target_pairs={{16,32},{32,16},{48,64},{64,48},{80,96},{96,80},{0,112},{112,0},{1... | collective-permute-start | bytes 786440 | tf_op jit(solution)/shard_map/ppermute | solution.py:254

commit v4 on v3

--- a/solution.py
+++ b/solution.py
@@ -20,28 +20,47 @@
 NT = (((1,), (1,)), ((), ()))
 VMEM = pl.BlockSpec(memory_space=pltpu.VMEM)
 SMEM = pl.BlockSpec(memory_space=pltpu.SMEM)
+ANY = pl.BlockSpec(memory_space=pl.ANY)
 
 
 def dot(a, b, dims=NN):
     return lax.dot_general(a, b, dims, preferred_element_type=F32)
 
 
-def pack_pairs(first_ref, second_ref, out_ref, rows):
+def pack_pairs(first_ref, second_ref, out_ref):
     for head in range(HEADS):
         lanes = slice(head * HEAD_DIM, (head + 1) * HEAD_DIM)
-        out_ref[head, rows] = jnp.concatenate([first_ref[:, lanes], second_ref[:, lanes]], axis=1)
-
-
-def pack_kernel(
-    lists_ref, counts_ref, key_ref, value_ref, query_ref, cot_ref, packed_ref, bias_ref
-):
+        out_ref[head] = jnp.concatenate([first_ref[:, lanes], second_ref[:, lanes]], axis=1)
+
+
+def pack_kernel(key_ref, value_ref, query_ref, cot_ref, packed_ref, held, pairs, in_sems, out_sems):
     cells = key_ref.shape[0]
-    pack_pairs(key_ref, value_ref, packed_ref, slice(0, cells))
-    pack_pairs(query_ref, cot_ref, packed_ref, slice(cells, 2 * cells))
+    arrivals = [
+        pltpu.make_async_copy(ref, held.at[i], in_sems.at[i])
+        for i, ref in enumerate((key_ref, value_ref, query_ref, cot_ref))
+    ]
+    for arrival in arrivals:
+        arrival.start()
+    departures = []
+    for i in range(2):
+        arrivals[2 * i].wait()
+        arrivals[2 * i + 1].wait()
+        rows = pl.ds(i * cells, cells)
+        pack_pairs(held.at[2 * i], held.at[2 * i + 1], pairs.at[i])
+        departures.append(
+            pltpu.make_async_copy(pairs.at[i], packed_ref.at[:, rows], out_sems.at[i])
+        )
+        departures[i].start()
+    for departure in departures:
+        departure.wait()
+
+
+def bias_kernel(lists_ref, counts_ref, bias_ref):
     band = lax.axis_index("lat")
     bands, slots = lists_ref.shape
     sectors = bias_ref.shape[0] - 2
     shape = (sectors, bias_ref.shape[1])
+    cells = shape[1] // sectors
     key_sector = lax.broadcasted_iota(jnp.int32, shape, 0)
     query_sector = lax.broadcasted_iota(jnp.int32, shape, 1) // cells
     offset = key_sector - query_sector
@@ -172,7 +191,7 @@
             far_grad_ref[first + a] = grad[cells:].astype(BF16)
         return carry
 
-    lax.fori_loop(0, chunks, chunk, 0)
+    lax.fori_loop(0, chunks, chunk, 0, unroll=True)
 
 
 def backward_kernel(
@@ -204,7 +223,7 @@
         out_ref[pl.ds(t * count, count)] = packed.T.reshape(count, cells, PAIR)
         return carry
 
-    lax.fori_loop(0, chunks, chunk, 0)
+    lax.fori_loop(0, chunks, chunk, 0, unroll=True)
 
 
 def merge_kernel(grad_ref, *refs):
@@ -260,12 +279,18 @@
             compiler_params=compiler_params, cost_estimate=cost(flops, 4 << 20), name=name,
         )(*args)
 
-    packed, bias = call(
-        pack_kernel,
-        (struct((HEADS, 2 * cells, PAIR), BF16), struct((sectors + 2, keys), F32)),
-        (neighbour_lists, list_counts)
-        + tuple(a.reshape(flat) for a in (key_vectors, value_vectors, queries, cotangent)),
-        "pack", 0, [SMEM] * 2 + [VMEM] * 4, compiler_params=None,
+    packed = pl.pallas_call(
+        pack_kernel, out_shape=struct((HEADS, 2 * cells, PAIR), BF16),
+        in_specs=[ANY] * 4, out_specs=ANY,
+        scratch_shapes=[
+            pltpu.VMEM((4,) + flat, BF16), pltpu.VMEM((2, HEADS, cells, PAIR), BF16),
+            pltpu.SemaphoreType.DMA((4,)), pltpu.SemaphoreType.DMA((2,)),
+        ],
+        cost_estimate=cost(0, 2 << 20), name="pack",
+    )(*(a.reshape(flat) for a in (key_vectors, value_vectors, queries, cotangent)))
+    (bias,) = call(
+        bias_kernel, (struct((sectors + 2, keys), F32),), (neighbour_lists, list_counts),
+        "bias", 10**8, [SMEM] * 2,
     )
     x = lax.all_to_all(packed, "lon", 0, 0, tiled=True)
     near = [(band, band ^ 1) for band in range(bands)]

time: 87 us -> 85.8 us (0.986)
  blocking collectives: 50.1 us -> 24.4 us
  waiting for transfers between devices: 1.61 us -> 18.2 us
  starting transfers between devices: 9.18 us -> 18.5 us
  local copies, waits for them, and re-layouts: 0.94 us -> 0.03 us
    all_to_all x1 -> x0, blocking collectives: 26 us -> none  [per_device(): x = lax.all_to_all(packed, 'lon', 0, 0, tiled=True)]
    all_to_all x0 -> x1, waiting for transfers between devices: none -> 16.4 us  [per_device(): x = lax.all_to_all(packed, 'lon', 0, 0, tiled=True)]
    all_to_all x0 -> x1, starting transfers between devices: none -> 9.31 us  [per_device(): x = lax.all_to_all(packed, 'lon', 0, 0, tiled=True)]
    pallas_call x9, Pallas kernels: 24.1 us -> 21.3 us  [call(): pl.pallas_call(kernel, out_shape=outs, in_specs=specs or [VMEM] * len(arg...]
    pallas_call x0 -> x1, Pallas kernels: none -> 2.32 us  [per_device(): pl.pallas_call(pack_kernel, out_shape=struct((HEADS, 2 * cells, PAIR), BF...]
    unnamed x2 -> x4, local copies, waits for them, and re-layouts: 0.93 us -> 0.01 us
  transfers between devices with their start and end apart: 8 -> 9, of which waited for: 1 -> 2; matrix products, arithmetic and copies ran while one was open for 0% -> 0% of each run, Pallas kernels for 23% -> 23%
where the time goes in v4:
time: 85.8 us; the launch traced here: 85.6 us
  blocking collectives  24.4 us (28%)
  Pallas kernels  23.6 us (28%)
  starting transfers between devices  18.5 us (22%)
  waiting for transfers between devices  18.2 us (21%)
    all_to_all x1, blocking collectives, per_device(): merged = lax.all_to_all(merged, 'lon', 0, 0, tiled=True)  24.4 us
    pallas_call x9, Pallas kernels, call(): pl.pallas_call(kernel, out_shape=outs, in_specs=specs or [VMEM] * len(arg...  21.3 us
    all_to_all x1, waiting for transfers between devices, per_device(): x = lax.all_to_all(packed, 'lon', 0, 0, tiled=True)  16.4 us
    all_to_all x1, starting transfers between devices, per_device(): x = lax.all_to_all(packed, 'lon', 0, 0, tiled=True)  9.31 us
    ppermute x4, starting transfers between devices, both_ways(): lax.ppermute(to_far, 'lat', far)  7.22 us
    pallas_call x1, Pallas kernels, per_device(): pl.pallas_call(pack_kernel, out_shape=struct((HEADS, 2 * cells, PAIR), BF...  2.32 us
    ppermute x4, starting transfers between devices, both_ways(): lax.ppermute(to_near, 'lat', near)  1.96 us
    ppermute x4, waiting for transfers between devices, both_ways(): lax.ppermute(to_far, 'lat', far)  1.8 us
  transfers between devices with their start and end apart: 9, of which 2 were waited for; matrix products, arithmetic and copies ran while one was open for 0% of the time, Pallas kernels for 23%

profile of v4, /device:TPU:1, one launch (start us, length us, event | category | flops | bytes accessed | tf_op | source)
XLA Modules:
  0.0 85.6 jit_solution(4363577579431559644)
XLA Ops:
  0.6 0.0 copy-start
  0.6 0.0 copy-start.1
  0.7 2.3 %pack.1 = bf16[16,256,128]{2,1,0:T(8,128)(2,1)} custom-call(bf16[128,1024]{1,0:T(8,128)(2,1)} %bitcast.8, bf16[128,1024]{1,0:T(8,128)(2,1)} %bitcast.9, bf16[128,1024]{1,0:T(8,128)(2,1)} %bitcast.10, bf16[128,1024]{1,0:T(8,128)(2,1)} %bitcast.11), custom_call_target="tpu_custom_call" | custom-call | bytes 2097152 | tf_op jit(solution)/shard_map/pack/pallas_call | solution.py:282
  3.0 9.3 %all-to-all-start = ((bf16[16,256,128]{2,1,0:T(8,128)(2,1)}), bf16[16,256,128]{2,1,0:T(8,128)(2,1)S(1)}, u32[]{:S(2)}, u32[]{:S(2)}) async-start(bf16[16,256,128]{2,1,0:T(8,128)(2,1)} %pack.1), calls=%async_computation | async-start | bytes 2097152 | tf_op jit(solution)/shard_map/all_to_all | solution.py:295
  12.3 0.0 copy-done
  12.3 0.8 bias.1.bias_ref
  13.1 16.4 %all-to-all-done.x_ref = bf16[16,256,128]{2,1,0:T(8,128)(2,1)S(1)} async-done(((bf16[16,256,128]{2,1,0:T(8,128)(2,1)}), bf16[16,256,128]{2,1,0:T(8,128)(2,1)S(1)}, u32[]{:S(2)}, u32[]{:S(2)}) %all-to-all-start) | async-done | bytes 1048608 | tf_op jit(solution)/shard_map/all_to_all | solution.py:295
  29.5 1.3 %collective-permute-start.2 = (bf16[8,128,128]{2,1,0:T(8,128)(2,1)S(1)}, bf16[8,128,128]{2,1,0:T(8,128)(2,1)S(1)}, u32[]{:S(2)}, u32[]{:S(2)}) collective-permute-start(bf16[8,128,128]{2,1,0:T(8,128)(2,1)S(1)} %slice.4), channel_id=1, source_target_pairs={{0,16},{16,0},{32,48},{48,32},{64,80},{80,64},{96,112},{112,96},{1... | collective-permute-start | bytes 786440 | tf_op jit(solution)/shard_map/ppermute | solution.py:273
  30.8 2.3 %collective-permute-start.3 = (bf16[8,128,128]{2,1,0:T(8,128)(2,1)S(1)}, bf16[8,128,128]{2,1,0:T(8,128)(2,1)S(1)}, u32[]{:S(2)}, u32[]{:S(2)}) collective-permute-start(bf16[8,128,128]{2,1,0:T(8,128)(2,1)S(1)} %slice.4), channel_id=1, source_target_pairs={{16,32},{32,16},{48,64},{64,48},{80,96},{96,80},{0,112},{112,0},{1... | collective-permute-start | bytes 786440 | tf_op jit(solution)/shard_map/ppermute | solution.py:273
  33.1 3.6 %forward.2 = (bf16[2,2048,512]{2,1,0:T(8,128)(2,1)S(1)}, f32[2,1,512]{2,1,0:T(1,128)S(1)}, f32[2,1,512]{2,1,0:T(1,128)S(1)}, f32[2,64,512]{2,1,0:T(8,128)S(1)}, ...) custom-call(bf16[16,256,128]{2,1,0:T(8,128)(2,1)S(1)} %all-to-all-done.x_ref, f32[18,2048]{1,0:T(8,128)S(1)} %bias.1.bias_ref), custom_call_target="tpu_custom_call" | custom-call | flops 5000000000 | bytes 4194304 | tf_op jit(solution)/shard_map/forward/pallas_call | solution.py:276
  36.7 0.1 collective-permute-start
  36.8 1.4 %collective-permute-start.1 = (bf16[8,128,128]{2,1,0:T(8,128)(2,1)S(1)}, bf16[8,128,128]{2,1,0:T(8,128)(2,1)S(1)}, u32[]{:S(2)}, u32[]{:S(2)}) collective-permute-start(bf16[8,128,128]{2,1,0:T(8,128)(2,1)S(1)} %get-tuple-element.36), channel_id=1, source_target_pairs={{16,32},{32,16},{48,64},{64,48},{80,96},{96,80},{0,112},{112,0},{1... | collective-permute-start | bytes 786440 | tf_op jit(solution)/shard_map/ppermute | solution.py:273
  38.2 3.6 %forward.3 = (bf16[2,2048,512]{2,1,0:T(8,128)(2,1)S(1)}, f32[2,1,512]{2,1,0:T(1,128)S(1)}, f32[2,1,512]{2,1,0:T(1,128)S(1)}, f32[2,64,512]{2,1,0:T(8,128)S(1)}) custom-call(bf16[16,256,128]{2,1,0:T(8,128)(2,1)S(1)} %all-to-all-done.x_ref, f32[18,2048]{1,0:T(8,128)S(1)} %bias.1.bias_ref, bf16[128,2048]{1,0:T(8,128)(2,1)S(1)} %get-tuple-element.34.kv_t_ref), custom_call_target="tpu_custom_call" | custom-call | flops 5000000000 | bytes 4194304 | tf_op jit(solution)/shard_map/forward/pallas_call | solution.py:276
  41.7 0.0 collective-permute-done.2.near_ref
  41.8 0.0 collective-permute-done.3.far_ref
  41.8 1.7 %rims.2 = (bf16[2,64,512]{2,1,0:T(8,128)(2,1)S(1)}, bf16[2,64,512]{2,1,0:T(8,128)(2,1)S(1)}, f32[2,1,512]{2,1,0:T(1,128)S(1)}, f32[2,64,512]{2,1,0:T(8,128)S(1)}...) custom-call(bf16[16,256,128]{2,1,0:T(8,128)(2,1)S(1)} %all-to-all-done.x_ref, ...), custom_call_target="tpu_custom_call" | custom-call | flops 1000000000 | bytes 4194304 | tf_op jit(solution)/shard_map/rims/pallas_call | solution.py:276
  43.5 0.4 collective-permute-start.4
  43.9 2.3 %collective-permute-start.5 = (bf16[8,128,128]{2,1,0:T(8,128)(2,1)S(1)}, bf16[8,128,128]{2,1,0:T(8,128)(2,1)S(1)}, u32[]{:S(2)}, u32[]{:S(2)}) collective-permute-start(bf16[8,128,128]{2,1,0:T(8,128)(2,1)S(1)} %get-tuple-element.55), channel_id=1, source_target_pairs={{16,32},{32,16},{48,64},{64,48},{80,96},{96,80},{0,112},{112,0},{1... | collective-permute-start | bytes 786440 | tf_op jit(solution)/shard_map/ppermute | solution.py:273
  46.1 4.2 %backward.2 = (bf16[8,128,128]{2,1,0:T(8,128)(2,1)S(1)}, f32[16,128,128]{2,1,0:T(8,128)S(1)}) custom-call(bf16[16,256,128]{2,1,0:T(8,128)(2,1)S(1)} %all-to-all-done.x_ref, bf16[128,2048]{1,0:T(8,128)(2,1)S(1)} %get-tuple-element.34.kv_t_ref, bf16[2,2048,512]{2,1,0:T(8,128)(2,1)S(1)} %get-tuple-element.40.weights_ref, ...), custom_call_target="tpu_custom_call" | custom-call | flops 5000000000 | bytes 4194304 | tf_op jit(solution)/shard_map/backward/pallas_call | solution.py:276
  50.4 0.0 collective-permute-done.near_ref
  50.4 0.0 collective-permute-done.1.far_ref
  50.4 1.7 %rims.3 = (bf16[2,64,512]{2,1,0:T(8,128)(2,1)S(1)}, bf16[2,64,512]{2,1,0:T(8,128)(2,1)S(1)}, f32[2,1,512]{2,1,0:T(1,128)S(1)}, f32[2,64,512]{2,1,0:T(8,128)S(1)}...) custom-call(bf16[16,256,128]{2,1,0:T(8,128)(2,1)S(1)} %all-to-all-done.x_ref, ...), custom_call_target="tpu_custom_call" | custom-call | flops 1000000000 | bytes 4194304 | tf_op jit(solution)/shard_map/rims/pallas_call | solution.py:276
  52.1 0.2 collective-permute-start.6
  52.2 1.3 %collective-permute-start.7 = (bf16[8,128,128]{2,1,0:T(8,128)(2,1)S(1)}, bf16[8,128,128]{2,1,0:T(8,128)(2,1)S(1)}, u32[]{:S(2)}, u32[]{:S(2)}) collective-permute-start(bf16[8,128,128]{2,1,0:T(8,128)(2,1)S(1)} %get-tuple-element.59), channel_id=1, source_target_pairs={{16,32},{32,16},{48,64},{64,48},{80,96},{96,80},{0,112},{112,0},{1... | collective-permute-start | bytes 786440 | tf_op jit(solution)/shard_map/ppermute | solution.py:273
  53.5 0.0 collective-permute-done.4.refs_1_
  53.5 0.0 collective-permute-done.5.refs_2_
  53.5 4.2 %backward.3 = (bf16[8,128,128]{2,1,0:T(8,128)(2,1)S(1)}, f32[16,128,128]{2,1,0:T(8,128)S(1)}) custom-call(bf16[16,256,128]{2,1,0:T(8,128)(2,1)S(1)} %all-to-all-done.x_ref, bf16[128,2048]{1,0:T(8,128)(2,1)S(1)} %get-tuple-element.34.kv_t_ref, bf16[2,2048,512]{2,1,0:T(8,128)(2,1)S(1)} %get-tuple-element.35.weights_ref, ...), custom_call_target="tpu_custom_call" | custom-call | flops 5000000000 | bytes 4194304 | tf_op jit(solution)/shard_map/backward/pallas_call | solution.py:276
  57.8 0.0 collective-permute-done.6.refs_4_
  57.8 1.8 %collective-permute-done.7.refs_5_ = bf16[8,128,128]{2,1,0:T(8,128)(2,1)S(1)} collective-permute-done((bf16[8,128,128]{2,1,0:T(8,128)(2,1)S(1)}, bf16[8,128,128]{2,1,0:T(8,128)(2,1)S(1)}, u32[]{:S(2)}, u32[]{:S(2)}) %collective-permute-start.7) | collective-permute-done | bytes 262176 | tf_op jit(solution)/shard_map/ppermute | solution.py:273
  59.6 0.2 merge.1
  59.8 24.4 %all_to_all.10.merged_ref = bf16[16,256,128]{2,1,0:T(8,128)(2,1)S(1)} all-to-all(bf16[16,256,128]{2,1,0:T(8,128)(2,1)S(1)} %merge.1), channel_id=1, replica_groups=mesh['lat'=8,'lon'=16] {'lon'}, dimensions={0} | all-to-all | bytes 2097152 | tf_op jit(solution)/shard_map/all_to_all | solution.py:340
  84.2 1.3 %unpack.1 = (bf16[128,1024]{1,0:T(8,128)(2,1)}, bf16[128,1024]{1,0:T(8,128)(2,1)}, bf16[128,1024]{1,0:T(8,128)(2,1)}, bf16[128,1024]{1,0:T(8,128)(2,1)}) custom-call(bf16[16,256,128]{2,1,0:T(8,128)(2,1)S(1)} %all_to_all.10.merged_ref), custom_call_target="tpu_custom_call" | custom-call | bytes 4194304 | tf_op jit(solution)/shard_map/unpack/pallas_call | solution.py:276
  (2 shorter events, 0.0 us)
Async XLA Ops:
  0.6 11.7 %copy-start = (s32[8,16]{1,0:T(8,128)S(1)}, s32[8,16]{1,0:T(8,128)}, u32[]{:S(2)}) copy-start(s32[8,16]{1,0:T(8,128)} %lists_ref.1) | copy-start | bytes 1540
  0.6 11.7 %copy-start.1 = (s32[8]{0:T(128)S(1)}, s32[8]{0:T(128)}, u32[]{:S(2)}) copy-start(s32[8]{0:T(128)} %counts_ref.1) | copy-start | bytes 100
  3.0 26.5 %all-to-all-start = ((bf16[16,256,128]{2,1,0:T(8,128)(2,1)}), bf16[16,256,128]{2,1,0:T(8,128)(2,1)S(1)}, u32[]{:S(2)}, u32[]{:S(2)}) async-start(bf16[16,256,128]{2,1,0:T(8,128)(2,1)} %pack.1), calls=%async_computation | async-start | bytes 2097152 | tf_op jit(solution)/shard_map/all_to_all | solution.py:295
  29.5 12.2 %collective-permute-start.2 = (bf16[8,128,128]{2,1,0:T(8,128)(2,1)S(1)}, bf16[8,128,128]{2,1,0:T(8,128)(2,1)S(1)}, u32[]{:S(2)}, u32[]{:S(2)}) collective-permute-start(bf16[8,128,128]{2,1,0:T(8,128)(2,1)S(1)} %slice.4), channel_id=1, source_target_pairs={{0,16},{16,0},{32,48},{48,32},{64,80},{80,64},{96,112},{112,96},{1... | collective-permute-start | bytes 786440 | tf_op jit(solution)/shard_map/ppermute | solution.py:273
  30.8 10.9 %collective-permute-start.3 = (bf16[8,128,128]{2,1,0:T(8,128)(2,1)S(1)}, bf16[8,128,128]{2,1,0:T(8,128)(2,1)S(1)}, u32[]{:S(2)}, u32[]{:S(2)}) collective-permute-start(bf16[8,128,128]{2,1,0:T(8,128)(2,1)S(1)} %slice.4), channel_id=1, source_target_pairs={{16,32},{32,16},{48,64},{64,48},{80,96},{96,80},{0,112},{112,0},{1... | collective-permute-start | bytes 786440 | tf_op jit(solution)/shard_map/ppermute | solution.py:273
  36.7 13.6 %collective-permute-start = (bf16[8,128,128]{2,1,0:T(8,128)(2,1)S(1)}, bf16[8,128,128]{2,1,0:T(8,128)(2,1)S(1)}, u32[]{:S(2)}, u32[]{:S(2)}) collective-permute-start(bf16[8,128,128]{2,1,0:T(8,128)(2,1)S(1)} %get-tuple-element.36), channel_id=1, source_target_pairs={{0,16},{16,0},{32,48},{48,32},{64,80},{80,64},{96,112},{112,96},{1... | collective-permute-start | bytes 786440 | tf_op jit(solution)/shard_map/ppermute | solution.py:273
  36.8 13.6 %collective-permute-start.1 = (bf16[8,128,128]{2,1,0:T(8,128)(2,1)S(1)}, bf16[8,128,128]{2,1,0:T(8,128)(2,1)S(1)}, u32[]{:S(2)}, u32[]{:S(2)}) collective-permute-start(bf16[8,128,128]{2,1,0:T(8,128)(2,1)S(1)} %get-tuple-element.36), channel_id=1, source_target_pairs={{16,32},{32,16},{48,64},{64,48},{80,96},{96,80},{0,112},{112,0},{1... | collective-permute-start | bytes 786440 | tf_op jit(solution)/shard_map/ppermute | solution.py:273
  43.5 10.1 %collective-permute-start.4 = (bf16[8,128,128]{2,1,0:T(8,128)(2,1)S(1)}, bf16[8,128,128]{2,1,0:T(8,128)(2,1)S(1)}, u32[]{:S(2)}, u32[]{:S(2)}) collective-permute-start(bf16[8,128,128]{2,1,0:T(8,128)(2,1)S(1)} %get-tuple-element.54), channel_id=1, source_target_pairs={{0,16},{16,0},{32,48},{48,32},{64,80},{80,64},{96,112},{112,96},{1... | collective-permute-start | bytes 786440 | tf_op jit(solution)/shard_map/ppermute | solution.py:273
  43.9 9.7 %collective-permute-start.5 = (bf16[8,128,128]{2,1,0:T(8,128)(2,1)S(1)}, bf16[8,128,128]{2,1,0:T(8,128)(2,1)S(1)}, u32[]{:S(2)}, u32[]{:S(2)}) collective-permute-start(bf16[8,128,128]{2,1,0:T(8,128)(2,1)S(1)} %get-tuple-element.55), channel_id=1, source_target_pairs={{16,32},{32,16},{48,64},{64,48},{80,96},{96,80},{0,112},{112,0},{1... | collective-permute-start | bytes 786440 | tf_op jit(solution)/shard_map/ppermute | solution.py:273
  52.1 5.7 %collective-permute-start.6 = (bf16[8,128,128]{2,1,0:T(8,128)(2,1)S(1)}, bf16[8,128,128]{2,1,0:T(8,128)(2,1)S(1)}, u32[]{:S(2)}, u32[]{:S(2)}) collective-permute-start(bf16[8,128,128]{2,1,0:T(8,128)(2,1)S(1)} %get-tuple-element.58), channel_id=1, source_target_pairs={{0,16},{16,0},{32,48},{48,32},{64,80},{80,64},{96,112},{112,96},{1... | collective-permute-start | bytes 786440 | tf_op jit(solution)/shard_map/ppermute | solution.py:273
  52.2 7.3 %collective-permute-start.7 = (bf16[8,128,128]{2,1,0:T(8,128)(2,1)S(1)}, bf16[8,128,128]{2,1,0:T(8,128)(2,1)S(1)}, u32[]{:S(2)}, u32[]{:S(2)}) collective-permute-start(bf16[8,128,128]{2,1,0:T(8,128)(2,1)S(1)} %get-tuple-element.59), channel_id=1, source_target_pairs={{16,32},{32,16},{48,64},{64,48},{80,96},{96,80},{0,112},{112,0},{1... | collective-permute-start | bytes 786440 | tf_op jit(solution)/shard_map/ppermute | solution.py:273

commit v5 on v4

--- a/solution.py
+++ b/solution.py
@@ -14,6 +14,7 @@
 LOG2E = 1.4426950408889634
 MASKED = -1e30
 CHUNK = 4
+PLANS = ((((0, 0),),), (((0, 1), (1, 0), (1, 1)),))
 BF16 = jnp.bfloat16
 F32 = jnp.float32
 NN = (((1,), (0,)), ((), ()))
@@ -138,105 +139,127 @@
 ):
     sectors, both, _ = x_ref.shape
     cells = both // 2
-    chunks, _, wide = out_ref.shape
+    chunks, _, narrow = out_ref.shape
+    wide = chunks * narrow
     count = wide // cells
     parts = [slice(a * cells, (a + 1) * cells) for a in range(count)]
-
-    def chunk(t, carry):
-        lanes = pl.ds(pl.multiple_of((start + t) * wide, wide), wide)
-        first = t * count
-        qc_t = x_ref[pl.ds(start * count + first, count), cells:].reshape(wide, PAIR).T
-        zeros = jnp.zeros((HEAD_DIM, wide), BF16)
-        queries = jnp.concatenate([qc_t[:HEAD_DIM], zeros], axis=0)
-        rims = [
-            jnp.concatenate([near_ref[first + a], far_ref[first + a]], axis=0)
-            for a in range(count)
-        ]
-        rims_t = [rim.T for rim in rims]
-
-        def beside(values):
-            return jnp.concatenate(values, axis=1)
-
-        s = beside([dot(rim, queries[:, part]) for rim, part in zip(rims, parts)])
-        s = s.reshape(2, cells, wide) + bias_ref[sectors : sectors + 2, lanes].reshape(2, 1, wide)
-        s = s.reshape(2 * cells, wide)
-        own = highest_ref[t]
-        highest = jnp.maximum(own, jnp.max(fold_rows(s, jnp.max), axis=0, keepdims=True))
-        p = jnp.exp2((s - highest) * (SCALE * LOG2E))
-        p_low = p.astype(BF16)
-        ratio = jnp.exp2((own - highest) * (SCALE * LOG2E))
-        total = ratio * total_ref[t] + jnp.sum(fold_rows(p, jnp.sum), axis=0, keepdims=True)
-        inverse = 1.0 / total
-        rim_out = [dot(rim_t[HEAD_DIM:], p_low[:, part]) for rim_t, part in zip(rims_t, parts)]
-        out_t = out_ref[t] * ratio + beside(rim_out)
-        attended = (out_t * inverse).astype(BF16)
-        attended_ref[t] = attended
-        cot_t = qc_t[HEAD_DIM:].astype(F32) * inverse
-        own_cot = (cot_t * ratio).astype(BF16)
-        cot_ref[t] = own_cot
-        spread_ref[t] = jnp.sum(own_cot.astype(F32) * attended.astype(F32), axis=0, keepdims=True)
-        cot_t = cot_t.astype(BF16)
-        spread = jnp.sum(cot_t.astype(F32) * attended.astype(F32), axis=0, keepdims=True)
-        cots = jnp.concatenate([zeros, cot_t], axis=0)
-        product = beside([dot(rim, cots[:, part]) for rim, part in zip(rims, parts)])
-        slopes = (p * (product - spread)).astype(BF16)
-        query_ref[t] = beside(
-            [dot(rim_t[:HEAD_DIM], slopes[:, part]) for rim_t, part in zip(rims_t, parts)]
-        )
-        for a, part in enumerate(parts):
-            left = beside([p_low[:, part], slopes[:, part]])
-            right = beside([cots[:, part], queries[:, part]])
-            grad = dot(left, right, NT) * lane_scale()
-            near_grad_ref[first + a] = grad[:cells].astype(BF16)
-            far_grad_ref[first + a] = grad[cells:].astype(BF16)
-        return carry
-
-    lax.fori_loop(0, chunks, chunk, 0, unroll=True)
-
-
-def backward_kernel(
-    start, x_ref, kv_t_ref, weights_ref, attended_ref, cot_ref, spread_ref, query_ref, *refs
-):
-    *before, out_ref, grad_ref, slopes_scr = refs
+    first = start * (narrow // cells)
+
+    def beside(values):
+        return jnp.concatenate(values, axis=1)
+
+    def read(ref):
+        return beside([ref[t] for t in range(chunks)])
+
+    def write(ref, value):
+        for t in range(chunks):
+            ref[t] = value[:, t * narrow : (t + 1) * narrow]
+
+    qc_t = x_ref[first : first + count, cells:].reshape(wide, PAIR).T
+    zeros = jnp.zeros((HEAD_DIM, wide), BF16)
+    queries = jnp.concatenate([qc_t[:HEAD_DIM], zeros], axis=0)
+    rims = [jnp.concatenate([near_ref[a], far_ref[a]], axis=0) for a in range(count)]
+    rims_t = [rim.T for rim in rims]
+    bias = bias_ref[sectors : sectors + 2, first * cells : (first + count) * cells]
+    s = beside([dot(rim, queries[:, part]) for rim, part in zip(rims, parts)])
+    s = (s.reshape(2, cells, wide) + bias.reshape(2, 1, wide)).reshape(2 * cells, wide)
+    own = read(highest_ref)
+    highest = jnp.maximum(own, jnp.max(fold_rows(s, jnp.max), axis=0, keepdims=True))
+    p = jnp.exp2((s - highest) * (SCALE * LOG2E))
+    p_low = p.astype(BF16)
+    ratio = jnp.exp2((own - highest) * (SCALE * LOG2E))
+    total = ratio * read(total_ref) + jnp.sum(fold_rows(p, jnp.sum), axis=0, keepdims=True)
+    inverse = 1.0 / total
+    rim_out = [dot(rim_t[HEAD_DIM:], p_low[:, part]) for rim_t, part in zip(rims_t, parts)]
+    out_t = read(out_ref) * ratio + beside(rim_out)
+    attended = (out_t * inverse).astype(BF16)
+    write(attended_ref, attended)
+    cot_t = qc_t[HEAD_DIM:].astype(F32) * inverse
+    own_cot = (cot_t * ratio).astype(BF16)
+    write(cot_ref, own_cot)
+    own_spread = own_cot.astype(F32) * attended.astype(F32)
+    write(spread_ref, jnp.sum(own_spread, axis=0, keepdims=True))
+    cot_t = cot_t.astype(BF16)
+    spread = jnp.sum(cot_t.astype(F32) * attended.astype(F32), axis=0, keepdims=True)
+    cots = jnp.concatenate([zeros, cot_t], axis=0)
+    product = beside([dot(rim, cots[:, part]) for rim, part in zip(rims, parts)])
+    slopes = (p * (product - spread)).astype(BF16)
+    for a, part in enumerate(parts):
+        left = beside([p_low[:, part], slopes[:, part]])
+        right = beside([cots[:, part], queries[:, part]])
+        grad = dot(left, right, NT) * lane_scale()
+        near_grad_ref[a] = grad[:cells].astype(BF16)
+        far_grad_ref[a] = grad[cells:].astype(BF16)
+    query_t = [dot(rim_t[:HEAD_DIM], slopes[:, part]) for rim_t, part in zip(rims_t, parts)]
+    write(query_ref, beside(query_t))
+
+
+def backward_kernel(plan, steps, x_ref, kv_t_ref, *refs):
+    parts = 1 + max(part for part, _ in plan)
+    groups = [refs[5 * i : 5 * i + 5] for i in range(parts)]
+    *before, out_ref, grad_ref, slopes_scr = refs[5 * parts :]
     sectors, both, _ = x_ref.shape
     cells = both // 2
-    chunks, keys, wide = weights_ref.shape
+    _, keys, wide = slopes_scr.shape
+    count = wide // cells
     grad_ref[...] = before[0][...] if before else jnp.zeros_like(grad_ref)
-
-    def chunk(t, carry):
-        count = wide // cells
-        queries_t = x_ref[pl.ds((start + t) * count, count), cells:].reshape(wide, PAIR).T[:HEAD_DIM]
-        zeros = jnp.zeros((HEAD_DIM, wide), BF16)
+    zeros = jnp.zeros((HEAD_DIM, wide), BF16)
+
+    def load(part, t):
+        first = (part * steps + t) * count
+        queries_t = x_ref[first : first + count, cells:].reshape(wide, PAIR).T[:HEAD_DIM]
         queries = jnp.concatenate([queries_t, zeros], axis=0)
-        cots = jnp.concatenate([zeros, cot_ref[t]], axis=0)
-        spread = spread_ref[t]
-        for block in range(0, sectors, 2):
-            rows = slice(block * cells, (block + 2) * cells)
-            product = dot(x_ref[block : block + 2, :cells].reshape(2 * cells, PAIR), cots)
-            slopes = weights_ref[t, rows, :].astype(F32) * (product - spread)
-            slopes_scr[rows, :] = slopes.astype(BF16)
-        query_t = query_ref[t] + dot(kv_t_ref[:HEAD_DIM, :], slopes_scr[...])
-        left = jnp.concatenate([weights_ref[t], slopes_scr[...]], axis=1)
-        grad = dot(left, jnp.concatenate([cots, queries], axis=1), NT)
-        grad_ref[...] += grad.reshape(sectors, cells, PAIR)
+        cots = jnp.concatenate([zeros, groups[part][2][t]], axis=0)
+        return cots, jnp.concatenate([cots, queries], axis=1), groups[part][3][t]
+
+    def make_slopes(i, cots, spread, block):
+        part, t = plan[i]
+        rows = slice(block * cells, (block + 2) * cells)
+        product = dot(x_ref[block : block + 2, :cells].reshape(2 * cells, PAIR), cots)
+        slopes = groups[part][0][t, rows, :].astype(F32) * (product - spread)
+        slopes_scr[i % 2, rows, :] = slopes.astype(BF16)
+
+    def add_grads(i, right, rows):
+        part, t = plan[i]
+        left = jnp.concatenate([groups[part][0][t, rows, :], slopes_scr[i % 2, rows, :]], axis=1)
+        first, last = rows.start // cells, rows.stop // cells
+        grad_ref[first:last] += dot(left, right, NT).reshape(last - first, cells, PAIR)
+
+    def finish(i):
+        part, t = plan[i]
+        attended_ref, query_ref = groups[part][1], groups[part][4]
+        query_t = query_ref[t] + dot(kv_t_ref[:HEAD_DIM, :], slopes_scr[i % 2])
         packed = jnp.concatenate([(query_t * SCALE).astype(BF16), attended_ref[t]], axis=0)
-        out_ref[pl.ds(t * count, count)] = packed.T.reshape(count, cells, PAIR)
-        return carry
-
-    lax.fori_loop(0, chunks, chunk, 0, unroll=True)
+        out_ref[i * count : (i + 1) * count] = packed.T.reshape(count, cells, PAIR)
+
+    run = keys // 4
+    for i in range(len(plan) + 1):
+        if i > 0:
+            before_right = right
+        if i < len(plan):
+            cots, right, spread = load(*plan[i])
+        for step in range(4):
+            if i < len(plan):
+                for block in range(step * sectors // 4, (step + 1) * sectors // 4, 2):
+                    make_slopes(i, cots, spread, block)
+            if i > 0:
+                add_grads(i - 1, before_right, slice(step * run, (step + 1) * run))
+        if i < len(plan):
+            finish(i)
 
 
 def merge_kernel(grad_ref, *refs):
     *part_refs, merged_ref = refs
     cells = grad_ref.shape[1]
+    scale = lane_scale().reshape(1, 1, PAIR)
+    for start, near_ref, far_ref in ((0, *part_refs[:2]), (part_refs[0].shape[0], *part_refs[2:4])):
+        part = slice(start, start + near_ref.shape[0])
+        grad = grad_ref[part] * scale + near_ref[...].astype(F32) + far_ref[...].astype(F32)
+        merged_ref[part, cells:] = grad.astype(BF16)
     start = 0
-    for out_ref, near_ref, far_ref in zip(part_refs[::3], part_refs[1::3], part_refs[2::3]):
-        part = slice(start, start + out_ref.shape[0])
-        merged_ref[part, :cells] = out_ref[...]
-        grad = grad_ref[part] * lane_scale().reshape(1, 1, PAIR)
-        grad = grad + near_ref[...].astype(F32) + far_ref[...].astype(F32)
-        merged_ref[part, cells:] = grad.astype(BF16)
-        start = part.stop
+    for out_ref in part_refs[4:]:
+        merged_ref[start : start + out_ref.shape[0], :cells] = out_ref[...]
+        start += out_ref.shape[0]
 
 
 def unpack_kernel(merged_ref, attended_ref, query_ref, key_ref, value_ref):
@@ -318,24 +341,31 @@
     )
     forward.append((weights, stats))
     last = stats[0]
-    before, returned = (), []
+    groups, returned, outs, grad = (), (), (), ()
     for i, (weights, stats) in enumerate(forward):
         *for_queries, near_grad, far_grad = call(
             functools.partial(rims_kernel, i * steps),
             (tall_low, tall_low, row, tall, by_part, by_part),
             (x, bias) + rims[i] + tuple(stats) + (last,), "rims", 10**9,
         )
-        from_rims = both_ways(near_grad, far_grad)
-        out, grad = call(
-            functools.partial(backward_kernel, i * steps),
-            (by_part, struct((sectors, cells, PAIR), F32)),
-            (x, kv_t, weights) + tuple(for_queries) + before, "backward", 5 * 10**9,
-            scratch=[pltpu.VMEM((keys, wide), BF16)],
-        )
-        before, last = (grad,) + from_rims, out
-        returned += [out, *from_rims]
+        returned += both_ways(near_grad, far_grad)
+        groups += (weights, *for_queries)
+        for plan in PLANS[i]:
+            out, grad = call(
+                functools.partial(backward_kernel, plan, steps),
+                (
+                    struct((len(plan) * CHUNK, cells, PAIR), BF16),
+                    struct((sectors, cells, PAIR), F32),
+                ),
+                (x, kv_t) + groups + grad, "backward", 10**8,
+                scratch=[pltpu.VMEM((2, keys, wide), BF16)],
+            )
+            grad = (grad,)
+            outs += (out,)
+        last = out
     (merged,) = call(
-        merge_kernel, (struct((sectors, 2 * cells, PAIR), BF16),), (grad, *returned), "merge", 0
+        merge_kernel, (struct((sectors, 2 * cells, PAIR), BF16),), grad + returned + outs,
+        "merge", 0,
     )
     merged = lax.all_to_all(merged, "lon", 0, 0, tiled=True)
     results = call(unpack_kernel, (struct(flat, BF16),) * 4, (merged,), "unpack", 0)

time: 85.8 us -> 83.3 us (0.971)
  Pallas kernels: 23.6 us -> 22.5 us
  waiting for transfers between devices: 18.2 us -> 17.1 us
    ppermute x4, waiting for transfers between devices: 1.8 us -> 0.65 us  [both_ways(): lax.ppermute(to_far, 'lat', far)]
    pallas_call x9, Pallas kernels: 21.3 us -> 20.2 us  [call(): pl.pallas_call(kernel, out_shape=outs, in_specs=specs or [VMEM] * len(arg...]
  transfers between devices with their start and end apart: 9 -> 9, of which waited for: 2 -> 2; matrix products, arithmetic and copies ran while one was open for 0% -> 0% of each run, Pallas kernels for 23% -> 22%
where the time goes in v5:
time: 83.3 us; the launch traced here: 83.1 us
  blocking collectives  24.2 us (29%)
  Pallas kernels  22.5 us (27%)
  starting transfers between devices  18.5 us (22%)
  waiting for transfers between devices  17.1 us (21%)
    all_to_all x1, blocking collectives, per_device(): merged = lax.all_to_all(merged, 'lon', 0, 0, tiled=True)  24.2 us
    pallas_call x9, Pallas kernels, call(): pl.pallas_call(kernel, out_shape=outs, in_specs=specs or [VMEM] * len(arg...  20.2 us
    all_to_all x1, waiting for transfers between devices, per_device(): x = lax.all_to_all(packed, 'lon', 0, 0, tiled=True)  16.4 us
    all_to_all x1, starting transfers between devices, per_device(): x = lax.all_to_all(packed, 'lon', 0, 0, tiled=True)  9.31 us
    ppermute x4, starting transfers between devices, both_ways(): lax.ppermute(to_far, 'lat', far)  7.54 us
    pallas_call x1, Pallas kernels, per_device(): pl.pallas_call(pack_kernel, out_shape=struct((HEADS, 2 * cells, PAIR), BF...  2.32 us
  transfers between devices with their start and end apart: 9, of which 2 were waited for; matrix products, arithmetic and copies ran while one was open for 0% of the time, Pallas kernels for 22%

profile of v5, /device:TPU:1, one launch (start us, length us, event | category | flops | bytes accessed | tf_op | source)
XLA Modules:
  0.0 83.1 jit_solution(16709190385266928530)
XLA Ops:
  0.6 0.0 copy-start.1
  0.6 0.0 copy-start
  0.7 2.3 %pack.1 = bf16[16,256,128]{2,1,0:T(8,128)(2,1)} custom-call(bf16[128,1024]{1,0:T(8,128)(2,1)} %bitcast.8, bf16[128,1024]{1,0:T(8,128)(2,1)} %bitcast.9, bf16[128,1024]{1,0:T(8,128)(2,1)} %bitcast.10, bf16[128,1024]{1,0:T(8,128)(2,1)} %bitcast.11), custom_call_target="tpu_custom_call" | custom-call | bytes 2097152 | tf_op jit(solution)/shard_map/pack/pallas_call | solution.py:305
  3.0 9.3 %all-to-all-start = ((bf16[16,256,128]{2,1,0:T(8,128)(2,1)}), bf16[16,256,128]{2,1,0:T(8,128)(2,1)S(1)}, u32[]{:S(2)}, u32[]{:S(2)}) async-start(bf16[16,256,128]{2,1,0:T(8,128)(2,1)} %pack.1), calls=%async_computation | async-start | bytes 2097152 | tf_op jit(solution)/shard_map/all_to_all | solution.py:318
  12.3 0.0 copy-done.1
  12.3 0.8 bias.1.bias_ref
  13.1 16.4 %all-to-all-done.x_ref = bf16[16,256,128]{2,1,0:T(8,128)(2,1)S(1)} async-done(((bf16[16,256,128]{2,1,0:T(8,128)(2,1)}), bf16[16,256,128]{2,1,0:T(8,128)(2,1)S(1)}, u32[]{:S(2)}, u32[]{:S(2)}) %all-to-all-start) | async-done | bytes 1048608 | tf_op jit(solution)/shard_map/all_to_all | solution.py:318
  29.5 3.0 %collective-permute-start.1 = (bf16[8,128,128]{2,1,0:T(8,128)(2,1)S(1)}, bf16[8,128,128]{2,1,0:T(8,128)(2,1)S(1)}, u32[]{:S(2)}, u32[]{:S(2)}) collective-permute-start(bf16[8,128,128]{2,1,0:T(8,128)(2,1)S(1)} %slice.4), channel_id=1, source_target_pairs={{16,32},{32,16},{48,64},{64,48},{80,96},{96,80},{0,112},{112,0},{1... | collective-permute-start | bytes 786440 | tf_op jit(solution)/shard_map/ppermute | solution.py:296
  32.5 0.0 collective-permute-start
  32.5 3.6 %forward.2 = (bf16[2,2048,512]{2,1,0:T(8,128)(2,1)S(1)}, f32[2,1,512]{2,1,0:T(1,128)S(1)}, f32[2,1,512]{2,1,0:T(1,128)S(1)}, f32[2,64,512]{2,1,0:T(8,128)S(1)}, ...) custom-call(bf16[16,256,128]{2,1,0:T(8,128)(2,1)S(1)} %all-to-all-done.x_ref, f32[18,2048]{1,0:T(8,128)S(1)} %bias.1.bias_ref), custom_call_target="tpu_custom_call" | custom-call | flops 5000000000 | bytes 4194304 | tf_op jit(solution)/shard_map/forward/pallas_call | solution.py:299
  36.2 0.9 %collective-permute-start.3 = (bf16[8,128,128]{2,1,0:T(8,128)(2,1)S(1)}, bf16[8,128,128]{2,1,0:T(8,128)(2,1)S(1)}, u32[]{:S(2)}, u32[]{:S(2)}) collective-permute-start(bf16[8,128,128]{2,1,0:T(8,128)(2,1)S(1)} %get-tuple-element.45), channel_id=1, source_target_pairs={{16,32},{32,16},{48,64},{64,48},{80,96},{96,80},{0,112},{112,0},{1... | collective-permute-start | bytes 786440 | tf_op jit(solution)/shard_map/ppermute | solution.py:296
  37.0 0.8 collective-permute-start.2
  37.8 3.6 %forward.3 = (bf16[2,2048,512]{2,1,0:T(8,128)(2,1)S(1)}, f32[2,1,512]{2,1,0:T(1,128)S(1)}, f32[2,1,512]{2,1,0:T(1,128)S(1)}, f32[2,64,512]{2,1,0:T(8,128)S(1)}) custom-call(bf16[16,256,128]{2,1,0:T(8,128)(2,1)S(1)} %all-to-all-done.x_ref, f32[18,2048]{1,0:T(8,128)S(1)} %bias.1.bias_ref, bf16[128,2048]{1,0:T(8,128)(2,1)S(1)} %get-tuple-element.34.kv_t_ref), custom_call_target="tpu_custom_call" | custom-call | flops 5000000000 | bytes 4194304 | tf_op jit(solution)/shard_map/forward/pallas_call | solution.py:299
  41.4 0.0 collective-permute-done.1.far_ref
  41.4 0.0 collective-permute-done.near_ref
  41.4 1.2 %rims.2 = (bf16[2,64,512]{2,1,0:T(8,128)(2,1)S(1)}, bf16[2,64,512]{2,1,0:T(8,128)(2,1)S(1)}, f32[2,1,512]{2,1,0:T(1,128)S(1)}, f32[2,64,512]{2,1,0:T(8,128)S(1)}...) custom-call(bf16[16,256,128]{2,1,0:T(8,128)(2,1)S(1)} %all-to-all-done.x_ref, ...), custom_call_target="tpu_custom_call" | custom-call | flops 1000000000 | bytes 4194304 | tf_op jit(solution)/shard_map/rims/pallas_call | solution.py:299
  42.6 0.8 collective-permute-start.4
  43.4 2.8 %collective-permute-start.5 = (bf16[8,128,128]{2,1,0:T(8,128)(2,1)S(1)}, bf16[8,128,128]{2,1,0:T(8,128)(2,1)S(1)}, u32[]{:S(2)}, u32[]{:S(2)}) collective-permute-start(bf16[8,128,128]{2,1,0:T(8,128)(2,1)S(1)} %get-tuple-element.56), channel_id=1, source_target_pairs={{16,32},{32,16},{48,64},{64,48},{80,96},{96,80},{0,112},{112,0},{1... | collective-permute-start | bytes 786440 | tf_op jit(solution)/shard_map/ppermute | solution.py:296
  46.2 2.1 %backward.2 = (bf16[4,128,128]{2,1,0:T(8,128)(2,1)S(1)}, f32[16,128,128]{2,1,0:T(8,128)S(1)}) custom-call(bf16[16,256,128]{2,1,0:T(8,128)(2,1)S(1)} %all-to-all-done.x_ref, bf16[128,2048]{1,0:T(8,128)(2,1)S(1)} %get-tuple-element.34.kv_t_ref, bf16[2,2048,512]{2,1,0:T(8,128)(2,1)S(1)} %get-tuple-element.35.refs_0_, ...), custom_call_target="tpu_custom_call" | custom-call | flops 100000000 | bytes 4194304 | tf_op jit(solution)/shard_map/backward/pallas_call | solution.py:299
  48.3 0.0 collective-permute-done.3.far_ref
  48.3 0.0 collective-permute-done.2.near_ref
  48.3 1.2 %rims.3 = (bf16[2,64,512]{2,1,0:T(8,128)(2,1)S(1)}, bf16[2,64,512]{2,1,0:T(8,128)(2,1)S(1)}, f32[2,1,512]{2,1,0:T(1,128)S(1)}, f32[2,64,512]{2,1,0:T(8,128)S(1)}...) custom-call(bf16[16,256,128]{2,1,0:T(8,128)(2,1)S(1)} %all-to-all-done.x_ref, ...), custom_call_target="tpu_custom_call" | custom-call | flops 1000000000 | bytes 4194304 | tf_op jit(solution)/shard_map/rims/pallas_call | solution.py:299
  49.6 0.1 collective-permute-start.6
  49.7 0.9 %collective-permute-start.7 = (bf16[8,128,128]{2,1,0:T(8,128)(2,1)S(1)}, bf16[8,128,128]{2,1,0:T(8,128)(2,1)S(1)}, u32[]{:S(2)}, u32[]{:S(2)}) collective-permute-start(bf16[8,128,128]{2,1,0:T(8,128)(2,1)S(1)} %get-tuple-element.58), channel_id=1, source_target_pairs={{16,32},{32,16},{48,64},{64,48},{80,96},{96,80},{0,112},{112,0},{1... | collective-permute-start | bytes 786440 | tf_op jit(solution)/shard_map/ppermute | solution.py:296
  50.5 6.2 %backward.3 = (bf16[12,128,128]{2,1,0:T(8,128)(2,1)S(1)}, f32[16,128,128]{2,1,0:T(8,128)S(1)}) custom-call(bf16[16,256,128]{2,1,0:T(8,128)(2,1)S(1)} %all-to-all-done.x_ref, bf16[128,2048]{1,0:T(8,128)(2,1)S(1)} %get-tuple-element.34.kv_t_ref, bf16[2,2048,512]{2,1,0:T(8,128)(2,1)S(1)} %get-tuple-element.35.refs_0_, ...), custom_call_target="tpu_custom_call" | custom-call | flops 100000000 | bytes 4194304 | tf_op jit(solution)/shard_map/backward/pallas_call | solution.py:299
  56.7 0.0 collective-permute-done.4.refs_0_
  56.7 0.0 collective-permute-done.5.refs_1_
  56.7 0.0 collective-permute-done.6.refs_2_
  56.7 0.6 collective-permute-done.7.refs_3_
  57.4 0.2 merge.1
  57.6 24.2 %all_to_all.10.merged_ref = bf16[16,256,128]{2,1,0:T(8,128)(2,1)S(1)} all-to-all(bf16[16,256,128]{2,1,0:T(8,128)(2,1)S(1)} %merge.1), channel_id=1, replica_groups=mesh['lat'=8,'lon'=16] {'lon'}, dimensions={0} | all-to-all | bytes 2097152 | tf_op jit(solution)/shard_map/all_to_all | solution.py:370
  81.8 1.3 %unpack.1 = (bf16[128,1024]{1,0:T(8,128)(2,1)}, bf16[128,1024]{1,0:T(8,128)(2,1)}, bf16[128,1024]{1,0:T(8,128)(2,1)}, bf16[128,1024]{1,0:T(8,128)(2,1)}) custom-call(bf16[16,256,128]{2,1,0:T(8,128)(2,1)S(1)} %all_to_all.10.merged_ref), custom_call_target="tpu_custom_call" | custom-call | bytes 4194304 | tf_op jit(solution)/shard_map/unpack/pallas_call | solution.py:299
  (2 shorter events, 0.0 us)
Async XLA Ops:
  0.6 11.7 %copy-start.1 = (s32[8]{0:T(128)S(1)}, s32[8]{0:T(128)}, u32[]{:S(2)}) copy-start(s32[8]{0:T(128)} %counts_ref.1) | copy-start | bytes 100
  0.6 11.7 %copy-start = (s32[8,16]{1,0:T(8,128)S(1)}, s32[8,16]{1,0:T(8,128)}, u32[]{:S(2)}) copy-start(s32[8,16]{1,0:T(8,128)} %lists_ref.1) | copy-start | bytes 1540
  3.0 26.5 %all-to-all-start = ((bf16[16,256,128]{2,1,0:T(8,128)(2,1)}), bf16[16,256,128]{2,1,0:T(8,128)(2,1)S(1)}, u32[]{:S(2)}, u32[]{:S(2)}) async-start(bf16[16,256,128]{2,1,0:T(8,128)(2,1)} %pack.1), calls=%async_computation | async-start | bytes 2097152 | tf_op jit(solution)/shard_map/all_to_all | solution.py:318
  29.5 11.9 %collective-permute-start.1 = (bf16[8,128,128]{2,1,0:T(8,128)(2,1)S(1)}, bf16[8,128,128]{2,1,0:T(8,128)(2,1)S(1)}, u32[]{:S(2)}, u32[]{:S(2)}) collective-permute-start(bf16[8,128,128]{2,1,0:T(8,128)(2,1)S(1)} %slice.4), channel_id=1, source_target_pairs={{16,32},{32,16},{48,64},{64,48},{80,96},{96,80},{0,112},{112,0},{1... | collective-permute-start | bytes 786440 | tf_op jit(solution)/shard_map/ppermute | solution.py:296
  32.5 8.9 %collective-permute-start = (bf16[8,128,128]{2,1,0:T(8,128)(2,1)S(1)}, bf16[8,128,128]{2,1,0:T(8,128)(2,1)S(1)}, u32[]{:S(2)}, u32[]{:S(2)}) collective-permute-start(bf16[8,128,128]{2,1,0:T(8,128)(2,1)S(1)} %slice.4), channel_id=1, source_target_pairs={{0,16},{16,0},{32,48},{48,32},{64,80},{80,64},{96,112},{112,96},{1... | collective-permute-start | bytes 786440 | tf_op jit(solution)/shard_map/ppermute | solution.py:296
  36.2 12.2 %collective-permute-start.3 = (bf16[8,128,128]{2,1,0:T(8,128)(2,1)S(1)}, bf16[8,128,128]{2,1,0:T(8,128)(2,1)S(1)}, u32[]{:S(2)}, u32[]{:S(2)}) collective-permute-start(bf16[8,128,128]{2,1,0:T(8,128)(2,1)S(1)} %get-tuple-element.45), channel_id=1, source_target_pairs={{16,32},{32,16},{48,64},{64,48},{80,96},{96,80},{0,112},{112,0},{1... | collective-permute-start | bytes 786440 | tf_op jit(solution)/shard_map/ppermute | solution.py:296
  37.0 11.3 %collective-permute-start.2 = (bf16[8,128,128]{2,1,0:T(8,128)(2,1)S(1)}, bf16[8,128,128]{2,1,0:T(8,128)(2,1)S(1)}, u32[]{:S(2)}, u32[]{:S(2)}) collective-permute-start(bf16[8,128,128]{2,1,0:T(8,128)(2,1)S(1)} %get-tuple-element.45), channel_id=1, source_target_pairs={{0,16},{16,0},{32,48},{48,32},{64,80},{80,64},{96,112},{112,96},{1... | collective-permute-start | bytes 786440 | tf_op jit(solution)/shard_map/ppermute | solution.py:296
  42.6 14.1 %collective-permute-start.4 = (bf16[8,128,128]{2,1,0:T(8,128)(2,1)S(1)}, bf16[8,128,128]{2,1,0:T(8,128)(2,1)S(1)}, u32[]{:S(2)}, u32[]{:S(2)}) collective-permute-start(bf16[8,128,128]{2,1,0:T(8,128)(2,1)S(1)} %get-tuple-element.55), channel_id=1, source_target_pairs={{0,16},{16,0},{32,48},{48,32},{64,80},{80,64},{96,112},{112,96},{1... | collective-permute-start | bytes 786440 | tf_op jit(solution)/shard_map/ppermute | solution.py:296
  43.4 13.3 %collective-permute-start.5 = (bf16[8,128,128]{2,1,0:T(8,128)(2,1)S(1)}, bf16[8,128,128]{2,1,0:T(8,128)(2,1)S(1)}, u32[]{:S(2)}, u32[]{:S(2)}) collective-permute-start(bf16[8,128,128]{2,1,0:T(8,128)(2,1)S(1)} %get-tuple-element.56), channel_id=1, source_target_pairs={{16,32},{32,16},{48,64},{64,48},{80,96},{96,80},{0,112},{112,0},{1... | collective-permute-start | bytes 786440 | tf_op jit(solution)/shard_map/ppermute | solution.py:296
  49.6 7.2 %collective-permute-start.6 = (bf16[8,128,128]{2,1,0:T(8,128)(2,1)S(1)}, bf16[8,128,128]{2,1,0:T(8,128)(2,1)S(1)}, u32[]{:S(2)}, u32[]{:S(2)}) collective-permute-start(bf16[8,128,128]{2,1,0:T(8,128)(2,1)S(1)} %get-tuple-element.57), channel_id=1, source_target_pairs={{0,16},{16,0},{32,48},{48,32},{64,80},{80,64},{96,112},{112,96},{1... | collective-permute-start | bytes 786440 | tf_op jit(solution)/shard_map/ppermute | solution.py:296
  49.7 7.7 %collective-permute-start.7 = (bf16[8,128,128]{2,1,0:T(8,128)(2,1)S(1)}, bf16[8,128,128]{2,1,0:T(8,128)(2,1)S(1)}, u32[]{:S(2)}, u32[]{:S(2)}) collective-permute-start(bf16[8,128,128]{2,1,0:T(8,128)(2,1)S(1)} %get-tuple-element.58), channel_id=1, source_target_pairs={{16,32},{32,16},{48,64},{64,48},{80,96},{96,80},{0,112},{112,0},{1... | collective-permute-start | bytes 786440 | tf_op jit(solution)/shard_map/ppermute | solution.py:296

commit v6 on v5

--- a/solution.py
+++ b/solution.py
@@ -86,7 +86,10 @@
     return combine(values.reshape(values.shape[0] // 8, 8, values.shape[1]), axis=0)
 
 
-def forward_part(start, x_ref, bias_ref, kv_t_ref, weights_ref, highest_ref, total_ref, out_ref, scores):
+def forward_part(
+    start, x_ref, bias_ref, kv_t_ref, weights_ref, highest_ref, total_ref, out_ref, scores,
+    transpose=False,
+):
     sectors, both, _ = x_ref.shape
     cells = both // 2
     chunks, keys, wide = weights_ref.shape
@@ -114,6 +117,10 @@
         for rows in blocks:
             if t < chunks:
                 highest = score(t, queries, rows, highest)
+            if t == 0 and transpose:
+                block = rows.start // cells
+                pairs = x_ref[block : block + 2, :cells].reshape(2 * cells, PAIR)
+                kv_t_ref[:, rows] = pairs.T
             if t > 0:
                 p = jnp.exp2((scores[before, rows, :] - before_highest) * (SCALE * LOG2E))
                 total = total + fold_rows(p, jnp.sum)
@@ -129,8 +136,7 @@
     *outs, kv_t_ref, kv_ref, scores = refs
     cells = kv_ref.shape[1]
     kv_ref[...] = x_ref[kv_ref.shape[0] :, :cells]
-    kv_t_ref[...] = x_ref[:, :cells].reshape(kv_t_ref.shape[1], PAIR).T
-    forward_part(0, x_ref, bias_ref, kv_t_ref, *outs, scores)
+    forward_part(0, x_ref, bias_ref, kv_t_ref, *outs, scores, transpose=True)
 
 
 def rims_kernel(
@@ -262,17 +268,23 @@
         start += out_ref.shape[0]
 
 
-def unpack_kernel(merged_ref, attended_ref, query_ref, key_ref, value_ref):
+def unpack_kernel(merged_ref, attended_ref, query_ref, key_ref, value_ref, held, sems):
     cells = attended_ref.shape[0]
-    for head in range(0, HEADS, 2):
-        lanes = slice(head * HEAD_DIM, (head + 2) * HEAD_DIM)
-        for rows, first_ref, second_ref in (
-            (slice(0, cells), query_ref, attended_ref),
-            (slice(cells, 2 * cells), key_ref, value_ref),
-        ):
+    copies = []
+    for i, (first_ref, second_ref) in enumerate(((query_ref, attended_ref), (key_ref, value_ref))):
+        rows = slice(i * cells, (i + 1) * cells)
+        for head in range(0, HEADS, 2):
+            lanes = slice(head * HEAD_DIM, (head + 2) * HEAD_DIM)
             one, two = merged_ref[head, rows], merged_ref[head + 1, rows]
-            first_ref[:, lanes] = jnp.concatenate([one[:, :HEAD_DIM], two[:, :HEAD_DIM]], axis=1)
-            second_ref[:, lanes] = jnp.concatenate([one[:, HEAD_DIM:], two[:, HEAD_DIM:]], axis=1)
+            held[2 * i, :, lanes] = jnp.concatenate([one[:, :HEAD_DIM], two[:, :HEAD_DIM]], axis=1)
+            held[2 * i + 1, :, lanes] = jnp.concatenate(
+                [one[:, HEAD_DIM:], two[:, HEAD_DIM:]], axis=1
+            )
+        for j, ref in ((2 * i, first_ref), (2 * i + 1, second_ref)):
+            copies.append(pltpu.make_async_copy(held.at[j], ref, sems.at[j]))
+            copies[j].start()
+    for copy in copies:
+        copy.wait()
 
 
 def cost(flops, nbytes):
@@ -368,7 +380,11 @@
         "merge", 0,
     )
     merged = lax.all_to_all(merged, "lon", 0, 0, tiled=True)
-    results = call(unpack_kernel, (struct(flat, BF16),) * 4, (merged,), "unpack", 0)
+    results = pl.pallas_call(
+        unpack_kernel, out_shape=(struct(flat, BF16),) * 4, in_specs=[VMEM], out_specs=(ANY,) * 4,
+        scratch_shapes=[pltpu.VMEM((4,) + flat, BF16), pltpu.SemaphoreType.DMA((4,))],
+        compiler_params=params, cost_estimate=cost(0, 2 << 20), name="unpack",
+    )(merged)
     return tuple(result.reshape(queries.shape) for result in results)
 
 

time: 83.3 us -> 83.4 us (level)
    pallas_call x9 -> x8, Pallas kernels: 20.2 us -> 18.9 us  [call(): pl.pallas_call(kernel, out_shape=outs, in_specs=specs or [VMEM] * len(arg...]
    pallas_call x0 -> x1, Pallas kernels: none -> 1.22 us  [per_device(): pl.pallas_call(unpack_kernel, out_shape=(struct(flat, BF16),) * 4, in_spe...]
where the time goes in v6:
time: 83.4 us; the launch traced here: 83.2 us
  blocking collectives  24.2 us (29%)
  Pallas kernels  22.4 us (27%)
  starting transfers between devices  18.5 us (22%)
  waiting for transfers between devices  17.1 us (21%)
  between operations  0.95 us (1%)
    all_to_all x1, blocking collectives, per_device(): merged = lax.all_to_all(merged, 'lon', 0, 0, tiled=True)  24.2 us
    pallas_call x8, Pallas kernels, call(): pl.pallas_call(kernel, out_shape=outs, in_specs=specs or [VMEM] * len(arg...  18.9 us
    all_to_all x1, waiting for transfers between devices, per_device(): x = lax.all_to_all(packed, 'lon', 0, 0, tiled=True)  16.4 us
    all_to_all x1, starting transfers between devices, per_device(): x = lax.all_to_all(packed, 'lon', 0, 0, tiled=True)  9.31 us
    ppermute x4, starting transfers between devices, both_ways(): lax.ppermute(to_far, 'lat', far)  7.55 us
    pallas_call x1, Pallas kernels, per_device(): pl.pallas_call(pack_kernel, out_shape=struct((HEADS, 2 * cells, PAIR), BF...  2.32 us
  transfers between devices with their start and end apart: 9, of which 2 were waited for; matrix products, arithmetic and copies ran while one was open for 0% of the time, Pallas kernels for 22%

profile of v6, /device:TPU:1, one launch (start us, length us, event | category | flops | bytes accessed | tf_op | source)
XLA Modules:
  0.0 83.2 jit_solution(10644320848880406384)
XLA Ops:
  0.6 0.0 copy-start.1
  0.6 0.0 copy-start
  0.7 2.3 %pack.1 = bf16[16,256,128]{2,1,0:T(8,128)(2,1)} custom-call(bf16[128,1024]{1,0:T(8,128)(2,1)} %bitcast.8, bf16[128,1024]{1,0:T(8,128)(2,1)} %bitcast.9, bf16[128,1024]{1,0:T(8,128)(2,1)} %bitcast.10, bf16[128,1024]{1,0:T(8,128)(2,1)} %bitcast.11), custom_call_target="tpu_custom_call" | custom-call | bytes 2097152 | tf_op jit(solution)/shard_map/pack/pallas_call | solution.py:317
  3.0 9.3 %all-to-all-start = ((bf16[16,256,128]{2,1,0:T(8,128)(2,1)}), bf16[16,256,128]{2,1,0:T(8,128)(2,1)S(1)}, u32[]{:S(2)}, u32[]{:S(2)}) async-start(bf16[16,256,128]{2,1,0:T(8,128)(2,1)} %pack.1), calls=%async_computation | async-start | bytes 2097152 | tf_op jit(solution)/shard_map/all_to_all | solution.py:330
  12.3 0.0 copy-done.1
  12.3 0.8 bias.1.bias_ref
  13.1 16.4 %all-to-all-done.x_ref = bf16[16,256,128]{2,1,0:T(8,128)(2,1)S(1)} async-done(((bf16[16,256,128]{2,1,0:T(8,128)(2,1)}), bf16[16,256,128]{2,1,0:T(8,128)(2,1)S(1)}, u32[]{:S(2)}, u32[]{:S(2)}) %all-to-all-start) | async-done | bytes 1048608 | tf_op jit(solution)/shard_map/all_to_all | solution.py:330
  29.5 3.0 %collective-permute-start.1 = (bf16[8,128,128]{2,1,0:T(8,128)(2,1)S(1)}, bf16[8,128,128]{2,1,0:T(8,128)(2,1)S(1)}, u32[]{:S(2)}, u32[]{:S(2)}) collective-permute-start(bf16[8,128,128]{2,1,0:T(8,128)(2,1)S(1)} %slice.4), channel_id=1, source_target_pairs={{16,32},{32,16},{48,64},{64,48},{80,96},{96,80},{0,112},{112,0},{1... | collective-permute-start | bytes 786440 | tf_op jit(solution)/shard_map/ppermute | solution.py:308
  32.5 0.0 collective-permute-start
  32.5 3.6 %forward.2 = (bf16[2,2048,512]{2,1,0:T(8,128)(2,1)S(1)}, f32[2,1,512]{2,1,0:T(1,128)S(1)}, f32[2,1,512]{2,1,0:T(1,128)S(1)}, f32[2,64,512]{2,1,0:T(8,128)S(1)}, ...) custom-call(bf16[16,256,128]{2,1,0:T(8,128)(2,1)S(1)} %all-to-all-done.x_ref, f32[18,2048]{1,0:T(8,128)S(1)} %bias.1.bias_ref), custom_call_target="tpu_custom_call" | custom-call | flops 5000000000 | bytes 4194304 | tf_op jit(solution)/shard_map/forward/pallas_call | solution.py:311
  36.2 0.9 %collective-permute-start.3 = (bf16[8,128,128]{2,1,0:T(8,128)(2,1)S(1)}, bf16[8,128,128]{2,1,0:T(8,128)(2,1)S(1)}, u32[]{:S(2)}, u32[]{:S(2)}) collective-permute-start(bf16[8,128,128]{2,1,0:T(8,128)(2,1)S(1)} %get-tuple-element.45), channel_id=1, source_target_pairs={{16,32},{32,16},{48,64},{64,48},{80,96},{96,80},{0,112},{112,0},{1... | collective-permute-start | bytes 786440 | tf_op jit(solution)/shard_map/ppermute | solution.py:308
  37.0 0.8 collective-permute-start.2
  37.8 3.6 %forward.3 = (bf16[2,2048,512]{2,1,0:T(8,128)(2,1)S(1)}, f32[2,1,512]{2,1,0:T(1,128)S(1)}, f32[2,1,512]{2,1,0:T(1,128)S(1)}, f32[2,64,512]{2,1,0:T(8,128)S(1)}) custom-call(bf16[16,256,128]{2,1,0:T(8,128)(2,1)S(1)} %all-to-all-done.x_ref, f32[18,2048]{1,0:T(8,128)S(1)} %bias.1.bias_ref, bf16[128,2048]{1,0:T(8,128)(2,1)S(1)} %get-tuple-element.34.kv_t_ref), custom_call_target="tpu_custom_call" | custom-call | flops 5000000000 | bytes 4194304 | tf_op jit(solution)/shard_map/forward/pallas_call | solution.py:311
  41.4 0.0 collective-permute-done.1.far_ref
  41.4 0.0 collective-permute-done.near_ref
  41.4 1.2 %rims.2 = (bf16[2,64,512]{2,1,0:T(8,128)(2,1)S(1)}, bf16[2,64,512]{2,1,0:T(8,128)(2,1)S(1)}, f32[2,1,512]{2,1,0:T(1,128)S(1)}, f32[2,64,512]{2,1,0:T(8,128)S(1)}...) custom-call(bf16[16,256,128]{2,1,0:T(8,128)(2,1)S(1)} %all-to-all-done.x_ref, ...), custom_call_target="tpu_custom_call" | custom-call | flops 1000000000 | bytes 4194304 | tf_op jit(solution)/shard_map/rims/pallas_call | solution.py:311
  42.6 0.8 collective-permute-start.4
  43.4 2.8 %collective-permute-start.5 = (bf16[8,128,128]{2,1,0:T(8,128)(2,1)S(1)}, bf16[8,128,128]{2,1,0:T(8,128)(2,1)S(1)}, u32[]{:S(2)}, u32[]{:S(2)}) collective-permute-start(bf16[8,128,128]{2,1,0:T(8,128)(2,1)S(1)} %get-tuple-element.56), channel_id=1, source_target_pairs={{16,32},{32,16},{48,64},{64,48},{80,96},{96,80},{0,112},{112,0},{1... | collective-permute-start | bytes 786440 | tf_op jit(solution)/shard_map/ppermute | solution.py:308
  46.2 2.1 %backward.2 = (bf16[4,128,128]{2,1,0:T(8,128)(2,1)S(1)}, f32[16,128,128]{2,1,0:T(8,128)S(1)}) custom-call(bf16[16,256,128]{2,1,0:T(8,128)(2,1)S(1)} %all-to-all-done.x_ref, bf16[128,2048]{1,0:T(8,128)(2,1)S(1)} %get-tuple-element.34.kv_t_ref, bf16[2,2048,512]{2,1,0:T(8,128)(2,1)S(1)} %get-tuple-element.35.refs_0_, ...), custom_call_target="tpu_custom_call" | custom-call | flops 100000000 | bytes 4194304 | tf_op jit(solution)/shard_map/backward/pallas_call | solution.py:311
  48.3 0.0 collective-permute-done.3.far_ref
  48.3 0.0 collective-permute-done.2.near_ref
  48.3 1.2 %rims.3 = (bf16[2,64,512]{2,1,0:T(8,128)(2,1)S(1)}, bf16[2,64,512]{2,1,0:T(8,128)(2,1)S(1)}, f32[2,1,512]{2,1,0:T(1,128)S(1)}, f32[2,64,512]{2,1,0:T(8,128)S(1)}...) custom-call(bf16[16,256,128]{2,1,0:T(8,128)(2,1)S(1)} %all-to-all-done.x_ref, ...), custom_call_target="tpu_custom_call" | custom-call | flops 1000000000 | bytes 4194304 | tf_op jit(solution)/shard_map/rims/pallas_call | solution.py:311
  49.6 0.1 collective-permute-start.6
  49.7 0.9 %collective-permute-start.7 = (bf16[8,128,128]{2,1,0:T(8,128)(2,1)S(1)}, bf16[8,128,128]{2,1,0:T(8,128)(2,1)S(1)}, u32[]{:S(2)}, u32[]{:S(2)}) collective-permute-start(bf16[8,128,128]{2,1,0:T(8,128)(2,1)S(1)} %get-tuple-element.58), channel_id=1, source_target_pairs={{16,32},{32,16},{48,64},{64,48},{80,96},{96,80},{0,112},{112,0},{1... | collective-permute-start | bytes 786440 | tf_op jit(solution)/shard_map/ppermute | solution.py:308
  50.5 6.2 %backward.3 = (bf16[12,128,128]{2,1,0:T(8,128)(2,1)S(1)}, f32[16,128,128]{2,1,0:T(8,128)S(1)}) custom-call(bf16[16,256,128]{2,1,0:T(8,128)(2,1)S(1)} %all-to-all-done.x_ref, bf16[128,2048]{1,0:T(8,128)(2,1)S(1)} %get-tuple-element.34.kv_t_ref, bf16[2,2048,512]{2,1,0:T(8,128)(2,1)S(1)} %get-tuple-element.35.refs_0_, ...), custom_call_target="tpu_custom_call" | custom-call | flops 100000000 | bytes 4194304 | tf_op jit(solution)/shard_map/backward/pallas_call | solution.py:311
  56.7 0.0 collective-permute-done.4.refs_0_
  56.7 0.0 collective-permute-done.5.refs_1_
  56.7 0.0 collective-permute-done.6.refs_2_
  56.7 0.6 collective-permute-done.7.refs_3_
  57.4 0.2 merge.1
  57.6 24.2 %all_to_all.10.merged_ref = bf16[16,256,128]{2,1,0:T(8,128)(2,1)S(1)} all-to-all(bf16[16,256,128]{2,1,0:T(8,128)(2,1)S(1)} %merge.1), channel_id=1, replica_groups=mesh['lat'=8,'lon'=16] {'lon'}, dimensions={0} | all-to-all | bytes 2097152 | tf_op jit(solution)/shard_map/all_to_all | solution.py:382
  81.8 1.2 %unpack.1 = (bf16[128,1024]{1,0:T(8,128)(2,1)}, bf16[128,1024]{1,0:T(8,128)(2,1)}, bf16[128,1024]{1,0:T(8,128)(2,1)}, bf16[128,1024]{1,0:T(8,128)(2,1)}) custom-call(bf16[16,256,128]{2,1,0:T(8,128)(2,1)S(1)} %all_to_all.10.merged_ref), custom_call_target="tpu_custom_call" | custom-call | bytes 2097152 | tf_op jit(solution)/shard_map/unpack/pallas_call | solution.py:383
  (2 shorter events, 0.0 us)
Async XLA Ops:
  0.6 11.7 %copy-start.1 = (s32[8]{0:T(128)S(1)}, s32[8]{0:T(128)}, u32[]{:S(2)}) copy-start(s32[8]{0:T(128)} %counts_ref.1) | copy-start | bytes 100
  0.6 11.7 %copy-start = (s32[8,16]{1,0:T(8,128)S(1)}, s32[8,16]{1,0:T(8,128)}, u32[]{:S(2)}) copy-start(s32[8,16]{1,0:T(8,128)} %lists_ref.1) | copy-start | bytes 1540
  3.0 26.5 %all-to-all-start = ((bf16[16,256,128]{2,1,0:T(8,128)(2,1)}), bf16[16,256,128]{2,1,0:T(8,128)(2,1)S(1)}, u32[]{:S(2)}, u32[]{:S(2)}) async-start(bf16[16,256,128]{2,1,0:T(8,128)(2,1)} %pack.1), calls=%async_computation | async-start | bytes 2097152 | tf_op jit(solution)/shard_map/all_to_all | solution.py:330
  29.5 11.8 %collective-permute-start.1 = (bf16[8,128,128]{2,1,0:T(8,128)(2,1)S(1)}, bf16[8,128,128]{2,1,0:T(8,128)(2,1)S(1)}, u32[]{:S(2)}, u32[]{:S(2)}) collective-permute-start(bf16[8,128,128]{2,1,0:T(8,128)(2,1)S(1)} %slice.4), channel_id=1, source_target_pairs={{16,32},{32,16},{48,64},{64,48},{80,96},{96,80},{0,112},{112,0},{1... | collective-permute-start | bytes 786440 | tf_op jit(solution)/shard_map/ppermute | solution.py:308
  32.5 8.8 %collective-permute-start = (bf16[8,128,128]{2,1,0:T(8,128)(2,1)S(1)}, bf16[8,128,128]{2,1,0:T(8,128)(2,1)S(1)}, u32[]{:S(2)}, u32[]{:S(2)}) collective-permute-start(bf16[8,128,128]{2,1,0:T(8,128)(2,1)S(1)} %slice.4), channel_id=1, source_target_pairs={{0,16},{16,0},{32,48},{48,32},{64,80},{80,64},{96,112},{112,96},{1... | collective-permute-start | bytes 786440 | tf_op jit(solution)/shard_map/ppermute | solution.py:308
  36.2 12.2 %collective-permute-start.3 = (bf16[8,128,128]{2,1,0:T(8,128)(2,1)S(1)}, bf16[8,128,128]{2,1,0:T(8,128)(2,1)S(1)}, u32[]{:S(2)}, u32[]{:S(2)}) collective-permute-start(bf16[8,128,128]{2,1,0:T(8,128)(2,1)S(1)} %get-tuple-element.45), channel_id=1, source_target_pairs={{16,32},{32,16},{48,64},{64,48},{80,96},{96,80},{0,112},{112,0},{1... | collective-permute-start | bytes 786440 | tf_op jit(solution)/shard_map/ppermute | solution.py:308
  37.0 11.3 %collective-permute-start.2 = (bf16[8,128,128]{2,1,0:T(8,128)(2,1)S(1)}, bf16[8,128,128]{2,1,0:T(8,128)(2,1)S(1)}, u32[]{:S(2)}, u32[]{:S(2)}) collective-permute-start(bf16[8,128,128]{2,1,0:T(8,128)(2,1)S(1)} %get-tuple-element.45), channel_id=1, source_target_pairs={{0,16},{16,0},{32,48},{48,32},{64,80},{80,64},{96,112},{112,96},{1... | collective-permute-start | bytes 786440 | tf_op jit(solution)/shard_map/ppermute | solution.py:308
  42.6 14.1 %collective-permute-start.4 = (bf16[8,128,128]{2,1,0:T(8,128)(2,1)S(1)}, bf16[8,128,128]{2,1,0:T(8,128)(2,1)S(1)}, u32[]{:S(2)}, u32[]{:S(2)}) collective-permute-start(bf16[8,128,128]{2,1,0:T(8,128)(2,1)S(1)} %get-tuple-element.55), channel_id=1, source_target_pairs={{0,16},{16,0},{32,48},{48,32},{64,80},{80,64},{96,112},{112,96},{1... | collective-permute-start | bytes 786440 | tf_op jit(solution)/shard_map/ppermute | solution.py:308
  43.4 13.3 %collective-permute-start.5 = (bf16[8,128,128]{2,1,0:T(8,128)(2,1)S(1)}, bf16[8,128,128]{2,1,0:T(8,128)(2,1)S(1)}, u32[]{:S(2)}, u32[]{:S(2)}) collective-permute-start(bf16[8,128,128]{2,1,0:T(8,128)(2,1)S(1)} %get-tuple-element.56), channel_id=1, source_target_pairs={{16,32},{32,16},{48,64},{64,48},{80,96},{96,80},{0,112},{112,0},{1... | collective-permute-start | bytes 786440 | tf_op jit(solution)/shard_map/ppermute | solution.py:308
  49.6 7.2 %collective-permute-start.6 = (bf16[8,128,128]{2,1,0:T(8,128)(2,1)S(1)}, bf16[8,128,128]{2,1,0:T(8,128)(2,1)S(1)}, u32[]{:S(2)}, u32[]{:S(2)}) collective-permute-start(bf16[8,128,128]{2,1,0:T(8,128)(2,1)S(1)} %get-tuple-element.57), channel_id=1, source_target_pairs={{0,16},{16,0},{32,48},{48,32},{64,80},{80,64},{96,112},{112,96},{1... | collective-permute-start | bytes 786440 | tf_op jit(solution)/shard_map/ppermute | solution.py:308
  49.7 7.7 %collective-permute-start.7 = (bf16[8,128,128]{2,1,0:T(8,128)(2,1)S(1)}, bf16[8,128,128]{2,1,0:T(8,128)(2,1)S(1)}, u32[]{:S(2)}, u32[]{:S(2)}) collective-permute-start(bf16[8,128,128]{2,1,0:T(8,128)(2,1)S(1)} %get-tuple-element.58), channel_id=1, source_target_pairs={{16,32},{32,16},{48,64},{64,48},{80,96},{96,80},{0,112},{112,0},{1... | collective-permute-start | bytes 786440 | tf_op jit(solution)/shard_map/ppermute | solution.py:308
